TPU v7x, 32 devices: a whole 2x2x4 slice. The times are simulated.
32 devices in a mesh: orb: 4 (over z), space: 8 (over y, x, core).
Axes of the slice: x: 2, y: 2, z: 4, core: 2. Of those that a mesh axis runs over, the one named last changes fastest.
Arguments:
- orbitals: float32 [32, 128, 128], P('orb', 'space'), may hold values from 0 to 0.25
- points: float32 [3, 128, 128], P(None, 'space')
- quad_weight: float32 [128, 128], P('space'), may hold values from 0.5 to 2
- external: float32 [128, 128], P('space'), may hold values from -3 to 1
- screening: float32 [32], replicated, may hold values from 0.05 to 2
- level_index: int32 [32], P('orb'), may hold values from 0 to 31
- near_cells: int32 [128, 27], P('space'), may hold values from -1 to 127, as said below
- far_cells: int32 [128, 42], P('space'), may hold values from -1 to 127, as said below
Outputs:
- new_orbitals: float32 [32, 128, 128], P('orb', 'space')
- hartree: float32 [128, 128], P('space')
Inputs may be any that keep to these rules, and one draw needn't show every extreme that they name: `near_cells`: row t lists distinct cells in increasing order, then -1: every cell of its own plane whose first two box indices differ from those of t by at most one (t itself among them), the cells directly above and below t, and some of the other cells of the two adjacent planes whose first two box indices differ from those of t by at most one. Some row holds 27 cells. `far_cells`: row t lists in increasing order, then -1, all cells of the planes floor(t / 16) - 1 to floor(t / 16) + 1 that are not in row t of near_cells. Some row holds 42 cells.
All inputs are finite; a program needn't handle non-finite values.
Results may differ from a plain program's by a relative error of at most 0.0003.
Values sent between devices are 32-bit elements; how exact they have to be, the bound alone decides.
No kernel may reach another device: no remote copies, remote signals or barrier semaphores. Data moves between devices by JAX's collectives and lax.ppermute only.
A program may use at most 64 MiB of HBM per device.

v0:
```python
import math

import jax
import jax.numpy as jnp
from jax import lax
from jax.sharding import PartitionSpec as P

NODES = 4


cell_side = 0.25
soften = 6.25e-06
green_scale = -0.5 / math.pi


def padded(cells, sides, width):
    for axis, dim in sides:
        count = lax.axis_size(axis)
        ends = count - 1
        head = lax.slice_in_dim(cells, 0, width, axis=dim)
        tail = lax.slice_in_dim(cells, cells.shape[dim] - width, cells.shape[dim], axis=dim)
        cells = jnp.concatenate(
            [
                lax.ppermute(tail, axis, [(i, (i + 1) % count) for i in range(ends)]),
                cells,
                lax.ppermute(head, axis, [((i + 1) % count, i) for i in range(ends)]),
            ],
            axis=dim,
        )
    return cells


def cheb_nodes(node_count):
    indices = jnp.arange(node_count, dtype=jnp.int32).astype(jnp.float32)
    return jnp.cos((2.0 * indices + 1.0) * (math.pi / (2.0 * node_count)))


def lagrange(scaled, node_set, node_count):
    factors = []
    for outer_node in range(node_count):
        running = jnp.ones_like(scaled)
        for inner_node in range(node_count):
            if inner_node != outer_node:
                running = running * (
                    (scaled - node_set[inner_node]) / (node_set[outer_node] - node_set[inner_node])
                )
        factors.append(running)
    return jnp.stack(factors)


def anterp(locations, corners, extent):
    node_set = cheb_nodes(NODES)
    scaled = 2.0 * (locations - corners[:, :, None]) / extent[:, None, None] - 1.0
    basis_x = lagrange(scaled[0], node_set, NODES)
    basis_y = lagrange(scaled[1], node_set, NODES)
    basis_z = lagrange(scaled[2], node_set, NODES)
    weights = basis_x[:, None, None] * basis_y[None, :, None] * basis_z[None, None, :]
    return weights.reshape((NODES * NODES * NODES,) + locations.shape[1:])


def proxies(corners, extent):
    node_set = cheb_nodes(NODES)
    offset = 0.5 * (node_set + 1.0)
    grid_shape = (NODES, NODES, NODES) + corners.shape[1:]
    grid_x = jnp.broadcast_to(
        (corners[0][None, :] + offset[:, None] * extent[0])[:, None, None], grid_shape
    )
    grid_y = jnp.broadcast_to(
        (corners[1][None, :] + offset[:, None] * extent[1])[None, :, None], grid_shape
    )
    grid_z = jnp.broadcast_to(
        (corners[2][None, :] + offset[:, None] * extent[2])[None, None, :], grid_shape
    )
    stacked = jnp.stack([grid_x, grid_y, grid_z]).reshape(
        (3, NODES * NODES * NODES) + corners.shape[1:]
    )
    return jnp.moveaxis(stacked, 1, 2)


def cell_lows(cell_ids):
    return (
        jnp.stack([cell_ids % 4, cell_ids // 4 % 4, cell_ids // 16]).astype(jnp.float32) * cell_side
    )


def plane_lows(levels):
    zeroes = jnp.zeros_like(levels)
    return jnp.stack([zeroes, zeroes, levels]).astype(jnp.float32) * cell_side


def cell_extent():
    return jnp.full((3,), cell_side, jnp.float32)


def plane_extent():
    return jnp.array([4.0 * cell_side, 4.0 * cell_side, cell_side], jnp.float32)


def kernel_sum(targets, locations, values, decay_rates):
    squared = jnp.zeros((targets.shape[1], locations.shape[1]), jnp.float32)
    for component in range(3):
        difference = targets[component][:, None] - locations[component][None, :]
        squared = squared + difference * difference
    distance = jnp.sqrt(squared + soften)
    kernel = jnp.exp(-decay_rates[:, None, None] * distance[None]) / distance[None]
    return jnp.sum(kernel * values[:, None, :], axis=2)


def cell_moments(mapping, values):
    return jnp.einsum("pcj,rcj->rcp", mapping, values, precision=lax.Precision.HIGHEST)


def plane_moments(mapping, values):
    grouped = values.reshape(values.shape[0], mapping.shape[1], -1)
    return jnp.einsum("pgj,rgj->rgp", mapping, grouped, precision=lax.Precision.HIGHEST)


def evaluate(
    targets,
    first_cell,
    target_offset,
    rim_points,
    rim_values,
    rim_mom,
    plane_proxy,
    plane_mom,
    near_cells,
    far_cells,
    decay_rates,
):
    kinds = rim_values.shape[0]
    levels = jnp.arange(plane_mom.shape[1], dtype=jnp.int32)
    extent = cell_extent()
    rim_base = first_cell - 16

    def per_cell(index):
        near_ids = near_cells[index]
        near_live = (near_ids >= 0).astype(jnp.float32)
        near_slot = jnp.where(near_ids >= 0, near_ids - rim_base, 0)
        near_src = rim_points[:, near_slot, :].reshape(3, -1)
        near_val = (rim_values[:, near_slot, :] * near_live[None, :, None]).reshape(kinds, -1)
        far_ids = far_cells[index]
        far_live = (far_ids >= 0).astype(jnp.float32)
        far_slot = jnp.where(far_ids >= 0, far_ids - rim_base, 0)
        far_src = proxies(cell_lows(jnp.maximum(far_ids, 0)), extent).reshape(3, -1)
        far_val = (rim_mom[:, far_slot, :] * far_live[None, :, None]).reshape(kinds, -1)
        plane_keep = (jnp.abs(levels - (first_cell + target_offset + index) // 16) >= 2).astype(
            jnp.float32
        )
        coarse_val = (plane_mom * plane_keep[None, :, None]).reshape(kinds, -1)
        points_here = targets[:, index, :]
        return (
            kernel_sum(points_here, near_src, near_val, decay_rates)
            + kernel_sum(points_here, far_src, far_val, decay_rates)
            + kernel_sum(points_here, plane_proxy, coarse_val, decay_rates)
        )

    count = targets.shape[1]
    group = 2 if count % 2 == 0 else 1
    grouped = jnp.arange(count, dtype=jnp.int32).reshape(count // group, group)
    result = lax.map(jax.vmap(per_cell), grouped)
    return result.reshape((count,) + result.shape[2:])


def body(orbitals, points, quad_weight, external, screening, level_index, near_cells, far_cells):
    cell_dev = orbitals.shape[1]
    point_count = orbitals.shape[2]
    spaces = lax.axis_size("space")
    first_cell = lax.axis_index("space") * cell_dev
    plane_dev = cell_dev // 16
    planes = plane_dev * spaces
    weight = quad_weight * (cell_side**3 / point_count)
    partial_value = 2.0 * jnp.sum(orbitals * orbitals, axis=0)
    density = lax.psum(partial_value, "orb")
    own_levels = first_cell // 16 + jnp.arange(plane_dev, dtype=jnp.int32)
    plane_map = anterp(points.reshape(3, plane_dev, -1), plane_lows(own_levels), plane_extent())
    levels = jnp.arange(planes, dtype=jnp.int32)
    plane_proxy = proxies(plane_lows(levels), plane_extent()).reshape(3, -1)
    rim_ids = first_cell - 16 + jnp.arange(cell_dev + 32, dtype=jnp.int32)
    charge = (weight * density)[None]
    charge_plane = plane_moments(plane_map, charge)
    rim_points, rim_charge = (
        padded(points, (("space", 1),), 16),
        padded(charge, (("space", 1),), 16),
    )
    rim_map = anterp(rim_points, cell_lows(rim_ids), cell_extent())
    rim_charge_mom = cell_moments(rim_map, rim_charge)
    all_charge_planes = lax.all_gather(charge_plane, "space", axis=1, tiled=True)
    no_decay = jnp.zeros((1,), jnp.float32)
    share_cells = cell_dev // lax.axis_size("orb")
    share_start = lax.axis_index("orb") * share_cells
    targets = lax.dynamic_slice_in_dim(points, share_start, share_cells, 1)
    near_share = lax.dynamic_slice_in_dim(near_cells, share_start, share_cells, 0)
    far_share = lax.dynamic_slice_in_dim(far_cells, share_start, share_cells, 0)
    partial_field = evaluate(
        targets,
        first_cell,
        share_start,
        rim_points,
        rim_charge,
        rim_charge_mom,
        plane_proxy,
        all_charge_planes,
        near_share,
        far_share,
        no_decay,
    )[:, 0, :]
    hartree = lax.all_gather(partial_field, "orb", axis=0, tiled=True)
    potential = external + hartree
    sources = (weight * potential)[None] * orbitals
    source_plane = plane_moments(plane_map, sources)
    rim_sources = padded(sources, (("space", 1),), 16)
    rim_source_mom = cell_moments(rim_map, rim_sources)
    all_source_planes = lax.all_gather(source_plane, "space", axis=1, tiled=True)
    level_match = (
        level_index[:, None] == jnp.arange(screening.shape[0], dtype=jnp.int32)[None, :]
    ).astype(jnp.float32)
    decay_rates = jnp.sum(level_match * screening[None, :], axis=1)
    updated = green_scale * evaluate(
        points,
        first_cell,
        0,
        rim_points,
        rim_sources,
        rim_source_mom,
        plane_proxy,
        all_source_planes,
        near_cells,
        far_cells,
        decay_rates,
    )
    return (jnp.transpose(updated, (1, 0, 2)), hartree)


def solution(mesh):
    in_specs = (
        P("orb", "space", None),
        P(None, "space", None),
        P("space", None),
        P("space", None),
        P(),
        P("orb"),
        P("space", None),
        P("space", None),
    )
    out_specs = (P("orb", "space", None), P("space", None))
    return jax.shard_map(body, mesh=mesh, in_specs=in_specs, out_specs=out_specs, check_vma=False)
```

profile of v0, /device:TPU:4, one launch (start us, length us, event | category | flops | bytes accessed | tf_op | source)
XLA Modules:
  0.0 311.2 jit_solution(2823218672820242113)
XLA Ops:
  0.7 1.9 collective-permute-start
  2.6 4.5 %collective-permute-start.1 = (f32[3,16,128]{2,1,0:T(8,128)}, f32[3,16,128]{2,1,0:T(8,128)S(1)}, u32[]{:S(2)}, u32[]{:S(2)}) collective-permute-start(f32[3,16,128]{2,1,0:T(8,128)} %param.15), channel_id=1, source_target_pairs={{1,0},{2,1},{3,2},{4,3},{5,4},{6,5},{7,6},{9,8},{10,9},{11,10},{12... | collective-permute-start | bytes 73736 | tf_op jit(solution)/shard_map/ppermute | solution.py:26
  7.1 0.9 multiply_reduce_fusion.6
  8.0 12.1 %psum.7 = f32[16,128]{1,0:T(8,128)S(1)} all-reduce(f32[16,128]{1,0:T(8,128)S(1)} %broadcast_multiply_fusion.9), channel_id=1, replica_groups=mesh['orb'=4,'space'=8] {'orb'}, use_global_device_ids=true, to_apply=%region_1.0 | all-reduce | flops 2048 | bytes 16384 | tf_op jit(solution)/shard_map/psum | solution.py:174
  20.8 1.9 collective-permute-start.3
  22.7 2.4 collective-permute-start.2
  45.2 2.5 divide_multiply_fusion.30
  47.7 2.5 divide_multiply_fusion.34
  53.9 13.9 %all-reduce.3 = f32[512]{0:T(512)S(1)} all-reduce(f32[512]{0:T(512)S(1)} %dynamic-update-slice), channel_id=2, replica_groups=mesh['orb'=4,'space'=8] {'space'}, use_global_device_ids=true, to_apply=%add.3 | all-reduce | flops 512 | bytes 4096
  68.2 2.5 divide_multiply_fusion.8
  70.7 1.9 divide_multiply_fusion.2
  72.6 2.5 divide_multiply_fusion.11
  75.8 2.6 fusion.32
  78.4 22.4 %while.30 = (s32[]{:T(128)}, f32[2,2,1,128]{3,1,2,0:T(2,128)S(1)}, s32[2,2]{1,0:T(2,128)S(1)}, f32[3,4,128]{2,0,1:T(4,128)S(1)}, s32[4,27]{1,0:T(4,128)S(1)}, /*...) while((s32[]{:T(128)}, f32[2,2,1,128]{3,1,2,0:T(2,128)S(1)}, ...), condition=%wide.wide.region_6.7_spmd.clone, body=%wide.wide.region_2.6_spmd.clone.sunk | while | flops 22204300 | bytes 1980101 | solution.py:161
  82.2 3.0 multiply_reduce_fusion.20
  87.3 2.2 multiply_reduce_fusion.21
  93.3 3.0 multiply_reduce_fusion.20
  98.5 2.2 multiply_reduce_fusion.21
  100.8 11.9 %all-gather.2 = f32[4,4,128]{2,1,0:T(4,128)S(1)} all-gather(f32[1,4,128]{2,1,0:T(4,128)S(1)} %bitcast.443), channel_id=1, replica_groups=mesh['orb'=4,'space'=8] {'orb'}, dimensions={0}, use_global_device_ids=true | all-gather | bytes 10240 | tf_op jit(solution)/shard_map/all_gather | solution.py:208
  112.7 1.9 collective-permute-start.5
  114.6 2.4 collective-permute-start.4
  117.5 8.6 %all-gather.3 = f32[8,64,8]{1,2,0:T(8,128)S(1)} all-gather(f32[1,64,8]{1,2,0:T(8,128)S(1)} %convolution_bitcast_fusion.1), channel_id=3, replica_groups=mesh['orb'=4,'space'=8] {'space'}, dimensions={0}, use_global_device_ids=true | all-gather | bytes 18432 | tf_op jit(solution)/shard_map/all_gather | solution.py:214
  126.4 2.5 convolution_bitcast_fusion
  129.0 180.9 %while.31 = (s32[]{:T(128)}, f32[8,2,8,128]{3,2,1,0:T(8,128)S(1)}, f32[1,8,1,1]{1,3,2,0:T(1,128)S(1)}, s32[8,2]{1,0:T(8,128)S(1)}, f32[3,16,128]{2,0,1:T(4,128)S...) while((s32[]{:T(128)}, f32[8,2,8,128]{3,2,1,0:T(8,128)S(1)}, ...), condition=%wide.wide.region_12.13_spmd.clone, body=%wide.wide.region_8.12_spmd.clone.sunk | while | flops 70005904 | bytes 18098988 | solution.py:161
  130.4 1.0 multiply_reduce_fusion.22
  133.6 2.5 add_sqrt_fusion.10
  136.1 6.4 %multiply_reduce_fusion.23 = f32[2,8,128]{2,1,0:T(8,128)S(1)} fusion(f32[2,8,3456]{2,1,0:T(8,128)S(1)} %broadcast_multiply_fusion.20, f32[2,128,3456]{2,1,0:T(8,128)S(1)} %add_sqrt_fusion.10, f32[8]{0:T(128)S(1)} %bitcast.445), kind=kLoop, calls=%fused_computation.70.clone.clone.1 | loop fusion | flops 28309504 | bytes 3768352 | tf_op jit(solution)/shard_map/while/body/eval_jaxpr/vmap()/reduce_sum | solution.py:106
  144.8 2.1 add_sqrt_fusion.11
  146.9 4.8 %multiply_reduce_fusion.24 = f32[2,8,128]{2,1,0:T(8,128)S(1)} fusion(f32[2,8,2688]{2,1,0:T(8,128)S(1)} %broadcast_multiply_fusion.21, f32[2,128,2688]{2,1,0:T(8,128)S(1)} %add_sqrt_fusion.11, f32[8]{0:T(128)S(1)} %bitcast.446), kind=kLoop, calls=%fused_computation.71.clone.clone.1 | loop fusion | flops 22018048 | bytes 2932768 | tf_op jit(solution)/shard_map/while/body/eval_jaxpr/vmap()/reduce_sum | solution.py:106
  153.0 1.0 multiply_reduce_fusion.22
  156.2 2.5 add_sqrt_fusion.10
  158.7 6.4 %multiply_reduce_fusion.23 = f32[2,8,128]{2,1,0:T(8,128)S(1)} fusion(f32[2,8,3456]{2,1,0:T(8,128)S(1)} %broadcast_multiply_fusion.20, f32[2,128,3456]{2,1,0:T(8,128)S(1)} %add_sqrt_fusion.10, f32[8]{0:T(128)S(1)} %bitcast.445), kind=kLoop, calls=%fused_computation.70.clone.clone.1 | loop fusion | flops 28309504 | bytes 3768352 | tf_op jit(solution)/shard_map/while/body/eval_jaxpr/vmap()/reduce_sum | solution.py:106
  167.4 2.1 add_sqrt_fusion.11
  169.5 4.8 %multiply_reduce_fusion.24 = f32[2,8,128]{2,1,0:T(8,128)S(1)} fusion(f32[2,8,2688]{2,1,0:T(8,128)S(1)} %broadcast_multiply_fusion.21, f32[2,128,2688]{2,1,0:T(8,128)S(1)} %add_sqrt_fusion.11, f32[8]{0:T(128)S(1)} %bitcast.446), kind=kLoop, calls=%fused_computation.71.clone.clone.1 | loop fusion | flops 22018048 | bytes 2932768 | tf_op jit(solution)/shard_map/while/body/eval_jaxpr/vmap()/reduce_sum | solution.py:106
  175.6 1.0 multiply_reduce_fusion.22
  178.8 2.5 add_sqrt_fusion.10
  181.3 6.4 %multiply_reduce_fusion.23 = f32[2,8,128]{2,1,0:T(8,128)S(1)} fusion(f32[2,8,3456]{2,1,0:T(8,128)S(1)} %broadcast_multiply_fusion.20, f32[2,128,3456]{2,1,0:T(8,128)S(1)} %add_sqrt_fusion.10, f32[8]{0:T(128)S(1)} %bitcast.445), kind=kLoop, calls=%fused_computation.70.clone.clone.1 | loop fusion | flops 28309504 | bytes 3768352 | tf_op jit(solution)/shard_map/while/body/eval_jaxpr/vmap()/reduce_sum | solution.py:106
  190.0 2.1 add_sqrt_fusion.11
  192.1 4.8 %multiply_reduce_fusion.24 = f32[2,8,128]{2,1,0:T(8,128)S(1)} fusion(f32[2,8,2688]{2,1,0:T(8,128)S(1)} %broadcast_multiply_fusion.21, f32[2,128,2688]{2,1,0:T(8,128)S(1)} %add_sqrt_fusion.11, f32[8]{0:T(128)S(1)} %bitcast.446), kind=kLoop, calls=%fused_computation.71.clone.clone.1 | loop fusion | flops 22018048 | bytes 2932768 | tf_op jit(solution)/shard_map/while/body/eval_jaxpr/vmap()/reduce_sum | solution.py:106
  198.2 1.0 multiply_reduce_fusion.22
  201.4 2.5 add_sqrt_fusion.10
  203.9 6.4 %multiply_reduce_fusion.23 = f32[2,8,128]{2,1,0:T(8,128)S(1)} fusion(f32[2,8,3456]{2,1,0:T(8,128)S(1)} %broadcast_multiply_fusion.20, f32[2,128,3456]{2,1,0:T(8,128)S(1)} %add_sqrt_fusion.10, f32[8]{0:T(128)S(1)} %bitcast.445), kind=kLoop, calls=%fused_computation.70.clone.clone.1 | loop fusion | flops 28309504 | bytes 3768352 | tf_op jit(solution)/shard_map/while/body/eval_jaxpr/vmap()/reduce_sum | solution.py:106
  212.6 2.1 add_sqrt_fusion.11
  214.7 4.8 %multiply_reduce_fusion.24 = f32[2,8,128]{2,1,0:T(8,128)S(1)} fusion(f32[2,8,2688]{2,1,0:T(8,128)S(1)} %broadcast_multiply_fusion.21, f32[2,128,2688]{2,1,0:T(8,128)S(1)} %add_sqrt_fusion.11, f32[8]{0:T(128)S(1)} %bitcast.446), kind=kLoop, calls=%fused_computation.71.clone.clone.1 | loop fusion | flops 22018048 | bytes 2932768 | tf_op jit(solution)/shard_map/while/body/eval_jaxpr/vmap()/reduce_sum | solution.py:106
  220.8 1.0 multiply_reduce_fusion.22
  224.0 2.5 add_sqrt_fusion.10
  226.5 6.4 %multiply_reduce_fusion.23 = f32[2,8,128]{2,1,0:T(8,128)S(1)} fusion(f32[2,8,3456]{2,1,0:T(8,128)S(1)} %broadcast_multiply_fusion.20, f32[2,128,3456]{2,1,0:T(8,128)S(1)} %add_sqrt_fusion.10, f32[8]{0:T(128)S(1)} %bitcast.445), kind=kLoop, calls=%fused_computation.70.clone.clone.1 | loop fusion | flops 28309504 | bytes 3768352 | tf_op jit(solution)/shard_map/while/body/eval_jaxpr/vmap()/reduce_sum | solution.py:106
  235.2 2.1 add_sqrt_fusion.11
  237.3 4.8 %multiply_reduce_fusion.24 = f32[2,8,128]{2,1,0:T(8,128)S(1)} fusion(f32[2,8,2688]{2,1,0:T(8,128)S(1)} %broadcast_multiply_fusion.21, f32[2,128,2688]{2,1,0:T(8,128)S(1)} %add_sqrt_fusion.11, f32[8]{0:T(128)S(1)} %bitcast.446), kind=kLoop, calls=%fused_computation.71.clone.clone.1 | loop fusion | flops 22018048 | bytes 2932768 | tf_op jit(solution)/shard_map/while/body/eval_jaxpr/vmap()/reduce_sum | solution.py:106
  243.4 1.0 multiply_reduce_fusion.22
  246.6 2.5 add_sqrt_fusion.10
  249.1 6.4 %multiply_reduce_fusion.23 = f32[2,8,128]{2,1,0:T(8,128)S(1)} fusion(f32[2,8,3456]{2,1,0:T(8,128)S(1)} %broadcast_multiply_fusion.20, f32[2,128,3456]{2,1,0:T(8,128)S(1)} %add_sqrt_fusion.10, f32[8]{0:T(128)S(1)} %bitcast.445), kind=kLoop, calls=%fused_computation.70.clone.clone.1 | loop fusion | flops 28309504 | bytes 3768352 | tf_op jit(solution)/shard_map/while/body/eval_jaxpr/vmap()/reduce_sum | solution.py:106
  257.8 2.1 add_sqrt_fusion.11
  259.9 4.8 %multiply_reduce_fusion.24 = f32[2,8,128]{2,1,0:T(8,128)S(1)} fusion(f32[2,8,2688]{2,1,0:T(8,128)S(1)} %broadcast_multiply_fusion.21, f32[2,128,2688]{2,1,0:T(8,128)S(1)} %add_sqrt_fusion.11, f32[8]{0:T(128)S(1)} %bitcast.446), kind=kLoop, calls=%fused_computation.71.clone.clone.1 | loop fusion | flops 22018048 | bytes 2932768 | tf_op jit(solution)/shard_map/while/body/eval_jaxpr/vmap()/reduce_sum | solution.py:106
  266.0 1.0 multiply_reduce_fusion.22
  269.2 2.5 add_sqrt_fusion.10
  271.7 6.4 %multiply_reduce_fusion.23 = f32[2,8,128]{2,1,0:T(8,128)S(1)} fusion(f32[2,8,3456]{2,1,0:T(8,128)S(1)} %broadcast_multiply_fusion.20, f32[2,128,3456]{2,1,0:T(8,128)S(1)} %add_sqrt_fusion.10, f32[8]{0:T(128)S(1)} %bitcast.445), kind=kLoop, calls=%fused_computation.70.clone.clone.1 | loop fusion | flops 28309504 | bytes 3768352 | tf_op jit(solution)/shard_map/while/body/eval_jaxpr/vmap()/reduce_sum | solution.py:106
  280.4 2.1 add_sqrt_fusion.11
  282.5 4.8 %multiply_reduce_fusion.24 = f32[2,8,128]{2,1,0:T(8,128)S(1)} fusion(f32[2,8,2688]{2,1,0:T(8,128)S(1)} %broadcast_multiply_fusion.21, f32[2,128,2688]{2,1,0:T(8,128)S(1)} %add_sqrt_fusion.11, f32[8]{0:T(128)S(1)} %bitcast.446), kind=kLoop, calls=%fused_computation.71.clone.clone.1 | loop fusion | flops 22018048 | bytes 2932768 | tf_op jit(solution)/shard_map/while/body/eval_jaxpr/vmap()/reduce_sum | solution.py:106
  288.6 1.0 multiply_reduce_fusion.22
  291.8 2.5 add_sqrt_fusion.10
  294.3 6.4 %multiply_reduce_fusion.23 = f32[2,8,128]{2,1,0:T(8,128)S(1)} fusion(f32[2,8,3456]{2,1,0:T(8,128)S(1)} %broadcast_multiply_fusion.20, f32[2,128,3456]{2,1,0:T(8,128)S(1)} %add_sqrt_fusion.10, f32[8]{0:T(128)S(1)} %bitcast.445), kind=kLoop, calls=%fused_computation.70.clone.clone.1 | loop fusion | flops 28309504 | bytes 3768352 | tf_op jit(solution)/shard_map/while/body/eval_jaxpr/vmap()/reduce_sum | solution.py:106
  303.0 2.1 add_sqrt_fusion.11
  305.1 4.8 %multiply_reduce_fusion.24 = f32[2,8,128]{2,1,0:T(8,128)S(1)} fusion(f32[2,8,2688]{2,1,0:T(8,128)S(1)} %broadcast_multiply_fusion.21, f32[2,128,2688]{2,1,0:T(8,128)S(1)} %add_sqrt_fusion.11, f32[8]{0:T(128)S(1)} %bitcast.446), kind=kLoop, calls=%fused_computation.71.clone.clone.1 | loop fusion | flops 22018048 | bytes 2932768 | tf_op jit(solution)/shard_map/while/body/eval_jaxpr/vmap()/reduce_sum | solution.py:106
  (567 shorter events, 68.0 us)
Async XLA Ops:
  0.6 51.8 %copy-start.8 = (u32[32]{0:T(128)S(1)}, u32[32]{0:T(128)}, u32[]{:S(2)}) copy-start(u32[32]{0:T(128)} %constant.577) | copy-start | bytes 388
  0.6 67.4 %copy-start.3 = (f32[3,16,128]{2,1,0:T(8,128)S(1)}, f32[3,16,128]{2,1,0:T(8,128)}, u32[]{:S(2)}) copy-start(f32[3,16,128]{2,1,0:T(8,128)} %param.15) | copy-start | bytes 73732
  0.7 67.3 %collective-permute-start = (f32[3,16,128]{2,1,0:T(8,128)}, f32[3,16,128]{2,1,0:T(8,128)S(1)}, u32[]{:S(2)}, u32[]{:S(2)}) collective-permute-start(f32[3,16,128]{2,1,0:T(8,128)} %param.15), channel_id=1, source_target_pairs={{0,1},{1,2},{2,3},{3,4},{4,5},{5,6},{6,7},{8,9},{9,10},{10,11},{11... | collective-permute-start | bytes 73736 | tf_op jit(solution)/shard_map/ppermute | solution.py:24
  2.6 65.4 %collective-permute-start.1 = (f32[3,16,128]{2,1,0:T(8,128)}, f32[3,16,128]{2,1,0:T(8,128)S(1)}, u32[]{:S(2)}, u32[]{:S(2)}) collective-permute-start(f32[3,16,128]{2,1,0:T(8,128)} %param.15), channel_id=1, source_target_pairs={{1,0},{2,1},{3,2},{4,3},{5,4},{6,5},{7,6},{9,8},{10,9},{11,10},{12... | collective-permute-start | bytes 73736 | tf_op jit(solution)/shard_map/ppermute | solution.py:26
  20.8 47.1 %collective-permute-start.3 = (f32[1,16,128]{2,1,0:T(8,128)S(1)}, f32[1,16,128]{2,1,0:T(8,128)S(1)}, u32[]{:S(2)}, u32[]{:S(2)}) collective-permute-start(f32[1,16,128]{2,1,0:T(8,128)S(1)} %bitcast.423), channel_id=1, source_target_pairs={{1,0},{2,1},{3,2},{4,3},{5,4},{6,5},{7,6},{9,8},{10,9},{11,10},{12... | collective-permute-start | bytes 24584 | tf_op jit(solution)/shard_map/ppermute | solution.py:26
  22.7 45.2 %collective-permute-start.2 = (f32[1,16,128]{2,1,0:T(8,128)S(1)}, f32[1,16,128]{2,1,0:T(8,128)S(1)}, u32[]{:S(2)}, u32[]{:S(2)}) collective-permute-start(f32[1,16,128]{2,1,0:T(8,128)S(1)} %bitcast.424), channel_id=1, source_target_pairs={{0,1},{1,2},{2,3},{3,4},{4,5},{5,6},{6,7},{8,9},{9,10},{10,11},{11... | collective-permute-start | bytes 24584 | tf_op jit(solution)/shard_map/ppermute | solution.py:24
  67.9 10.4 %copy-start.6 = (f32[1,8,64]{2,1,0:T(8,128)}, f32[1,8,64]{2,1,0:T(8,128)S(1)}, u32[]{:S(2)}) copy-start(f32[1,8,64]{2,1,0:T(8,128)S(1)} %reshape.1807) | copy-start | bytes 6148
  78.3 34.3 %copy-start.5 = (f32[16,128]{1,0:T(8,128)S(1)}, f32[16,128]{1,0:T(8,128)}, u32[]{:S(2)}) copy-start(f32[16,128]{1,0:T(8,128)} %param.16) | copy-start | bytes 24580
  78.3 34.3 %copy-start.7 = (f32[16,128]{1,0:T(8,128)S(1)}, f32[16,128]{1,0:T(8,128)}, u32[]{:S(2)}) copy-start(f32[16,128]{1,0:T(8,128)} %param.17) | copy-start | bytes 24580
  78.3 34.3 %copy-start = (f32[8,16,128]{2,1,0:T(8,128)S(1)}, f32[8,16,128]{2,1,0:T(8,128)}, u32[]{:S(2)}) copy-start(f32[8,16,128]{2,1,0:T(8,128)} %param.14) | copy-start | bytes 196612
  78.3 50.6 %copy-start.1 = (s32[16,27]{1,0:T(8,128)S(1)}, s32[16,27]{1,0:T(8,128)}, u32[]{:S(2)}) copy-start(s32[16,27]{1,0:T(8,128)} %param.20) | copy-start | bytes 5188
  78.4 50.6 %copy-start.2 = (s32[16,42]{1,0:T(8,128)S(1)}, s32[16,42]{1,0:T(8,128)}, u32[]{:S(2)}) copy-start(s32[16,42]{1,0:T(8,128)} %param.21) | copy-start | bytes 8068
  112.7 13.7 %collective-permute-start.5 = (f32[8,16,128]{2,0,1:T(8,128)S(1)}, f32[8,16,128]{2,0,1:T(8,128)S(1)}, u32[]{:S(2)}, u32[]{:S(2)}) collective-permute-start(f32[8,16,128]{2,0,1:T(8,128)S(1)} %copy_multiply_fusion), channel_id=1, source_target_pairs={{1,0},{2,1},{3,2},{4,3},{5,4},{6,5},{7,6},{9,8},{10,9},{11,10},{12... | collective-permute-start | bytes 196616 | tf_op jit(solution)/shard_map/ppermute | solution.py:26
  114.6 11.8 %collective-permute-start.4 = (f32[8,16,128]{2,0,1:T(8,128)S(1)}, f32[8,16,128]{2,0,1:T(8,128)S(1)}, u32[]{:S(2)}, u32[]{:S(2)}) collective-permute-start(f32[8,16,128]{2,0,1:T(8,128)S(1)} %copy_multiply_fusion), channel_id=1, source_target_pairs={{0,1},{1,2},{2,3},{3,4},{4,5},{5,6},{6,7},{8,9},{9,10},{10,11},{11... | collective-permute-start | bytes 196616 | tf_op jit(solution)/shard_map/ppermute | solution.py:24
  126.3 2.6 copy-start.4
where the time goes:
time: 314 us; the launch traced here: 311 us
  other arithmetic  170 us (54%)
  local copies, waits for them, and re-layouts  54.2 us (17%)
  blocking collectives  46.5 us (15%)
  between operations  16.3 us (5%)
  starting transfers between devices  15.1 us (5%)
  matrix products  6.12 us (2%)
    reduce_sum x30, other arithmetic, kernel_sum(): return jnp.sum(kernel * values[:, None, :], axis=2)  110 us
    sqrt x24, other arithmetic, kernel_sum(): distance = jnp.sqrt(squared + soften)  39.6 us
    unnamed x1, blocking collectives  13.9 us
    psum x1, blocking collectives, body(): density = lax.psum(partial_value, 'orb')  12.1 us
    mul x5, other arithmetic, lagrange(): running * ((scaled - node_set[inner_node]) / (node_set[outer_node] - node...  11.9 us
    all_gather x1, blocking collectives, body(): hartree = lax.all_gather(partial_field, 'orb', axis=0, tiled=True)  11.9 us
    all_gather x1, blocking collectives, body(): lax.all_gather(source_plane, 'space', axis=1, tiled=True)  8.61 us
    gather x28, local copies, waits for them, and re-layouts, per_cell(): rim_mom[:, far_slot, :] * far_live[None, :, None]  8.47 us
  transfers between devices with their start and end apart: 6, of which 0 were waited for; matrix products, arithmetic and copies ran while one was open for 5% of the time, Pallas kernels for 0%

commit v1 on v0

v1 whole, which is shorter than its diff:
```python
import functools
import math

import jax
import jax.numpy as jnp
import numpy as np
from jax import lax
from jax.experimental import pallas as pl
from jax.experimental.pallas import tpu as pltpu
from jax.sharding import PartitionSpec as P

NODES = 4
LANES = 128
PLANE = 16
ROWS = 8
HALF = NODES**3

cell_side = 0.25
soften = 6.25e-06
green_scale = -0.5 / math.pi
log2e = math.log2(math.e)
highest = lax.Precision.HIGHEST

node_set = np.cos((2.0 * np.arange(NODES) + 1.0) * (math.pi / (2.0 * NODES)))
roots = [[node_set[m] for m in range(NODES) if m != a] for a in range(NODES)]
scales = [1.0 / np.prod([node_set[a] - r for r in roots[a]]) for a in range(NODES)]


def basis_rows():
    row = np.arange(ROWS)
    out = []
    for pick in (row // 4, 2 + row // 4, row % 4):
        for k in range(NODES - 1):
            out.append([roots[a][k] for a in pick])
        out.append([scales[a] for a in pick])
    return np.broadcast_to(np.array(out, np.float32)[:, :, None], (12, ROWS, LANES)).copy()


def proxy_table(planes, window):
    offset = 0.5 * (node_set + 1.0)
    p = np.arange(LANES) % HALF
    offs = np.stack([offset[p // 16], offset[p // 4 % 4], offset[p % 4]])
    cells = np.arange(window)
    lows = np.stack([cells % 4, cells // 4 % 4, cells // 16]) * cell_side
    near = lows[:, :, None] + offs[:, None, :] * cell_side
    levels = np.arange(planes)
    lows = np.stack([0 * levels, 0 * levels, levels]) * cell_side
    far = lows[:, :, None] + offs[:, None, :] * np.array([1.0, 1.0, cell_side])[:, None, None]
    table = np.zeros((window + planes, ROWS, LANES), np.float32)
    table[:, :3] = np.moveaxis(np.concatenate([near, far], 1), 0, 1)
    return table


def poly(u, r0, r1, r2, scale):
    return ((u - r0) * (u - r1)) * ((u - r2) * scale)


def weights(cst, x, y, z, lows, sides):
    ux, uy, uz = (
        jnp.broadcast_to(2.0 * (c - lo) / e - 1.0, (ROWS, LANES)) for c, lo, e in zip((x, y, z), lows, sides)
    )
    pz = poly(uz, cst[8], cst[9], cst[10], cst[11])
    pyz = [poly(uy, cst[4 * k], cst[4 * k + 1], cst[4 * k + 2], cst[4 * k + 3]) * pz for k in range(2)]
    parts = []
    for a in range(NODES):
        px = poly(ux, *(float(r) for r in roots[a]), float(scales[a]))
        parts += [px * pyz[0], px * pyz[1]]
    return jnp.concatenate(parts + parts, axis=0)


def cell_low(cell):
    return [(cell % 4).astype(jnp.float32) * cell_side, (cell // 4 % 4).astype(jnp.float32) * cell_side]


def dot_nt(a, b):
    return lax.dot_general(a, b, (((1,), (1,)), ((), ())), precision=highest, preferred_element_type=jnp.float32)


def charge_kernel(meta, cst, own, density, out):
    z_low = meta[0].astype(jnp.float32) * cell_side
    cells = own.shape[0]

    def step(c, acc):
        charge = own[c, 4:5, :] * density[pl.ds(c, 1), :]
        out[pl.ds(c, 1), :] = charge
        w = weights(cst, own[c, 0:1, :], own[c, 1:2, :], own[c, 2:3, :], (0.0, 0.0, z_low), (1.0, 1.0, cell_side))
        return acc + w * charge

    acc = lax.fori_loop(0, cells, step, jnp.zeros((LANES, LANES), jnp.float32))
    out[cells:, :] = dot_nt(jnp.ones((ROWS, LANES), jnp.float32), acc)


def field(kinds, group, unroll, meta, counts, near, far, rate, table, win, val, mom, tgt, src, srcv, acc, write):
    cells = near.shape[0]
    window = win.shape[0]
    planes = table.shape[0] - window
    me = meta[0]
    base = me * cells - PLANE
    below = jnp.maximum(me - 1, 0)
    live_planes = below + jnp.maximum(planes - 2 - me, 0)
    low_half = lax.broadcasted_iota(jnp.int32, (1, LANES), 1) < HALF

    def per_cell(t, carry):
        n_near, n_far = counts[t, 0], counts[t, 1]
        n_items = n_far + live_planes

        def put_near(j, c):
            slot = near[t, j] - base
            src[j] = win[slot, :ROWS, :]
            srcv[j] = val[slot]
            return c

        lax.fori_loop(0, n_near, put_near, 0)

        def item(j):
            j = jnp.minimum(j, n_items - 1)
            p = j - n_far
            level = jnp.where(p < below, p, p + (me + 2 - below))
            cell = far[t, jnp.minimum(j, far.shape[1] - 1)] - base
            return jnp.where(j < n_far, cell, window + level)

        n_pairs = (n_items + 1) // 2

        def put_far(j, c):
            first, second = item(2 * j), item(2 * j + 1)
            live = (2 * j + 1 < n_items).astype(jnp.float32)
            src[n_near + j] = jnp.where(low_half, table[first], table[second])
            srcv[n_near + j] = jnp.where(low_half, mom[first], mom[second] * live)
            return c

        lax.fori_loop(0, n_pairs, put_far, 0)
        n_chunks = n_near + n_pairs
        for u in range(unroll - 1):
            src[n_chunks + u] = jnp.zeros(src.shape[1:], jnp.float32)
            srcv[n_chunks + u] = jnp.zeros(srcv.shape[1:], jnp.float32)
        for d in range(3):
            row = win[PLANE + t, d : d + 1, :]
            tgt[d] = jnp.broadcast_to(row, (LANES, LANES)).T

        height = group * ROWS

        def per_group(g, c):
            at = pl.multiple_of(g * height, height)
            tx, ty, tz = (tgt[d, pl.ds(at, height), :] for d in range(3))

            def step(k, accs):
                accs = list(accs)
                for u in range(unroll):
                    slot = k * unroll + u
                    dx = tx - src[slot, 0:1, :]
                    dy = ty - src[slot, 1:2, :]
                    dz = tz - src[slot, 2:3, :]
                    sq = (dx * dx + dy * dy) + (dz * dz + soften)
                    inv = lax.rsqrt(sq)
                    if rate is None:
                        accs[0] = accs[0] + inv * srcv[slot, 0:1, :]
                    else:
                        dist = sq * inv
                        for i in range(kinds):
                            accs[i] = accs[i] + (jnp.exp2(dist * rate[i]) * inv) * srcv[slot, i : i + 1, :]
                return tuple(accs)

            zero = jnp.zeros((height, LANES), jnp.float32)
            accs = lax.fori_loop(0, (n_chunks + unroll - 1) // unroll, step, (zero,) * kinds)
            for i in range(kinds):
                acc[i, pl.ds(at, height), :] = accs[i]
            return c

        lax.fori_loop(0, LANES // height, per_group, 0)
        ones = jnp.ones((ROWS, LANES), jnp.float32)
        for i in range(kinds):
            write(t, i, dot_nt(ones, acc[i])[0:1, :])
        return carry

    lax.fori_loop(0, cells, per_cell, 0)


def window_moments(cst, win, val, mom, me):
    kinds = val.shape[1]

    def step(c, carry):
        z_low = (me - 1 + c // PLANE).astype(jnp.float32) * cell_side
        w = weights(cst, win[c, 0:1, :], win[c, 1:2, :], win[c, 2:3, :], (*cell_low(c), z_low), (cell_side,) * 3)
        v = val[c]
        if kinds == 1:
            v = jnp.broadcast_to(v, (ROWS, LANES))
        mom[c] = dot_nt(v, w)[:kinds, :]
        return carry

    lax.fori_loop(0, win.shape[0], step, 0)


def plane_at(meta, g):
    return lax.bitwise_xor(meta[0], g)


def hartree_kernel(
    group, unroll, meta, counts, near, far, cst, table, win, gathered, out, val, mom, tgt, src, srcv, acc
):
    cells = near.shape[0]
    planes = gathered.shape[0]
    kinds = win.shape[1] - ROWS
    me = meta[0]
    for k in range(3):
        there = jnp.clip(me - 1 + k, 0, planes - 1)
        val[pl.ds(k * PLANE, PLANE), 0, :] = gathered[plane_at(meta, there), :PLANE, :]

    def put_plane(g, c):
        mom[win.shape[0] + g] = gathered[plane_at(meta, g), cells : cells + 1, :]
        return c

    lax.fori_loop(0, planes, put_plane, 0)
    window_moments(cst, win, val, mom, me)

    def write(t, i, row):
        out[pl.ds(t, 1), :] = row

    field(1, group, unroll, meta, counts, near, far, None, table, win, val, mom, tgt, src, srcv, acc, write)
    z_low = me.astype(jnp.float32) * cell_side

    def step(c, total):
        there = PLANE + c
        w = weights(
            cst, win[there, 0:1, :], win[there, 1:2, :], win[there, 2:3, :], (0.0, 0.0, z_low), (1.0, 1.0, cell_side)
        )
        v = win[there, ROWS:, :] * (win[there, 4:5, :] * (win[there, 3:4, :] + out[pl.ds(c, 1), :]))
        return total + dot_nt(v, w)

    out[cells:, :] = lax.fori_loop(0, cells, step, jnp.zeros((kinds, LANES), jnp.float32))


def orbital_kernel(
    group, unroll, meta, counts, near, far, rate, cst, table, win, gathered, out, val, mom, tgt, src, srcv, acc
):
    cells = near.shape[0]
    planes = gathered.shape[0]
    kinds = out.shape[0]
    me = meta[0]
    for k in range(3):
        there = plane_at(meta, jnp.clip(me - 1 + k, 0, planes - 1))

        def put(c, carry):
            at = k * PLANE + c
            scaled = win[at, 4:5, :] * (win[at, 3:4, :] + gathered[there, pl.ds(c, 1), :])
            val[at] = win[at, ROWS:, :] * scaled
            return carry

        lax.fori_loop(0, PLANE, put, 0)

    def put_plane(g, c):
        mom[win.shape[0] + g] = gathered[plane_at(meta, g), cells:, :]
        return c

    lax.fori_loop(0, planes, put_plane, 0)
    window_moments(cst, win, val, mom, me)

    def write(t, i, row):
        out[i, pl.ds(t, 1), :] = row * green_scale

    field(kinds, group, unroll, meta, counts, near, far, rate, table, win, val, mom, tgt, src, srcv, acc, write)


def gather_xor(block, axis):
    count = lax.axis_size(axis)
    out = block[None]
    bit = 1
    while bit < count:
        out = jnp.concatenate([out, lax.ppermute(out, axis, [(i, i ^ bit) for i in range(count)])], axis=0)
        bit *= 2
    return out


def sum_xor(value, axis):
    count = lax.axis_size(axis)
    bit = 1
    while bit < count:
        value = value + lax.ppermute(value, axis, [(i, i ^ bit) for i in range(count)])
        bit *= 2
    return value


def smem():
    return pl.BlockSpec(memory_space=pltpu.SMEM)


def vmem():
    return pl.BlockSpec(memory_space=pltpu.VMEM)


def scratch(kinds, window, planes, chunks):
    return [
        pltpu.VMEM((window, kinds, LANES), jnp.float32),
        pltpu.VMEM((window + planes, kinds, LANES), jnp.float32),
        pltpu.VMEM((3, LANES, LANES), jnp.float32),
        pltpu.VMEM((chunks, ROWS, LANES), jnp.float32),
        pltpu.VMEM((chunks, kinds, LANES), jnp.float32),
        pltpu.VMEM((kinds, LANES, LANES), jnp.float32),
    ]


def body(orbitals, points, quad_weight, external, screening, level_index, near_cells, far_cells):
    kinds, cells, point_count = orbitals.shape
    planes = lax.axis_size("space")
    window = cells + 2 * PLANE
    me = lax.axis_index("space")
    meta = jnp.full((1,), me, jnp.int32)
    params = pltpu.CompilerParams(vmem_limit_bytes=48 * 1024 * 1024)

    density = sum_xor(2.0 * jnp.sum(orbitals * orbitals, axis=0), "orb")
    weight = quad_weight * (cell_side**3 / point_count)
    own = jnp.concatenate(
        [
            jnp.transpose(points, (1, 0, 2)),
            external[:, None],
            weight[:, None],
            jnp.zeros((cells, 3, point_count), jnp.float32),
            jnp.transpose(orbitals, (1, 0, 2)),
        ],
        axis=1,
    )
    ends = planes - 1
    win = jnp.concatenate(
        [
            lax.ppermute(own, "space", [(i, i + 1) for i in range(ends)]),
            own,
            lax.ppermute(own, "space", [(i + 1, i) for i in range(ends)]),
        ],
        axis=0,
    )
    cst = jnp.asarray(basis_rows())
    base_table = proxy_table(planes, window)
    shift = np.zeros(base_table.shape, np.float32)
    shift[:window, 2] = cell_side
    table = jnp.asarray(base_table) + jnp.asarray(shift) * (me - 1).astype(jnp.float32)
    counts = jnp.stack(
        [jnp.sum((near_cells >= 0).astype(jnp.int32), 1), jnp.sum((far_cells >= 0).astype(jnp.int32), 1)], axis=1
    )
    level_match = level_index[:, None] == jnp.arange(screening.shape[0], dtype=jnp.int32)[None, :]
    rate = jnp.sum(jnp.where(level_match, screening[None, :], 0.0), axis=1) * (-log2e)

    charges = pl.pallas_call(
        charge_kernel,
        out_shape=jax.ShapeDtypeStruct((cells + ROWS, LANES), jnp.float32),
        in_specs=[smem(), vmem(), vmem(), vmem()],
        out_specs=vmem(),
        compiler_params=params,
        name="charge",
    )(meta, cst, own, density)
    charges = gather_xor(charges, "space")

    slots = near_cells.shape[1] + (far_cells.shape[1] + planes + 1) // 2
    group, unroll = 16, 2
    potentials = pl.pallas_call(
        functools.partial(hartree_kernel, group, unroll),
        out_shape=jax.ShapeDtypeStruct((cells + kinds, LANES), jnp.float32),
        in_specs=[smem()] * 4 + [vmem()] * 4,
        out_specs=vmem(),
        scratch_shapes=scratch(1, window, planes, slots + unroll),
        compiler_params=params,
        name="hartree",
    )(meta, counts, near_cells, far_cells, cst, table, win, charges)
    gathered = gather_xor(potentials, "space")

    group, unroll = 4, 4
    updated = pl.pallas_call(
        functools.partial(orbital_kernel, group, unroll),
        out_shape=jax.ShapeDtypeStruct((kinds, cells, LANES), jnp.float32),
        in_specs=[smem()] * 5 + [vmem()] * 4,
        out_specs=vmem(),
        scratch_shapes=scratch(kinds, window, planes, slots + unroll),
        compiler_params=params,
        name="orbitals",
    )(meta, counts, near_cells, far_cells, rate, cst, table, win, gathered)
    return updated, potentials[:cells]


def solution(mesh):
    in_specs = (
        P("orb", "space", None),
        P(None, "space", None),
        P("space", None),
        P("space", None),
        P(),
        P("orb"),
        P("space", None),
        P("space", None),
    )
    out_specs = (P("orb", "space", None), P("space", None))
    return jax.shard_map(body, mesh=mesh, in_specs=in_specs, out_specs=out_specs, check_vma=False)
```

time: 314 us -> 189 us (0.60)
  other arithmetic: 170 us -> 1.43 us
  Pallas kernels: 0 us -> 155 us
  local copies, waits for them, and re-layouts: 54.2 us -> 1.75 us
  blocking collectives: 46.5 us -> 0 us
  waiting for transfers between devices: 0.02 us -> 17.7 us
  between operations: 16.3 us -> 0.82 us
  matrix products: 6.12 us -> 0 us
  starting transfers between devices: 15.1 us -> 11.9 us
    pallas_call x0 -> x3, Pallas kernels: none -> 155 us  [the longest x1 108 us: body(): pl.pallas_call(functools.partial(orbital_kernel, group, unroll), out_shap...]
    reduce_sum x32 -> x4, other arithmetic: 111 us -> 1.32 us  [the longest x1 0.92 us: body(): density = sum_xor(2.0 * jnp.sum(orbitals * orbitals, axis=0), 'orb')]
    sqrt x24 -> x0, other arithmetic: 39.6 us -> none  [kernel_sum(): distance = jnp.sqrt(squared + soften)]
    gather x90 -> x0, local copies, waits for them, and re-layouts: 38.2 us -> none  [the longest x28 8.47 us: per_cell(): rim_mom[:, far_slot, :] * far_live[None, :, None]]
    all_gather x2 -> x0, blocking collectives: 20.5 us -> none  [the longest x1 11.9 us: body(): hartree = lax.all_gather(partial_field, 'orb', axis=0, tiled=True)]
    ppermute x6 -> x10, waiting for transfers between devices: 0.02 us -> 17.7 us  [the longest x6 15.8 us: gather_xor(): lax.ppermute(out, axis, [(i, i ^ bit) for i in range(count)])]
    mul x70 -> x3, other arithmetic: 14.7 us -> 0.01 us  [the longest x1 0.01 us: body(): density = sum_xor(2.0 * jnp.sum(orbitals * orbitals, axis=0), 'orb')]
    unnamed x1 -> x0, blocking collectives: 13.9 us -> none
  transfers between devices with their start and end apart: 6 -> 10, of which waited for: 0 -> 7; matrix products, arithmetic and copies ran while one was open for 5% -> 1% of each run, Pallas kernels for 0% -> 0%
where the time goes in v1:
time: 189 us
  Pallas kernels  155 us (82%)
  waiting for transfers between devices  17.7 us (9%)
  starting transfers between devices  11.9 us (6%)
    pallas_call x1, Pallas kernels, body(): pl.pallas_call(functools.partial(orbital_kernel, group, unroll), out_shap...  108 us
    pallas_call x1, Pallas kernels, body(): pl.pallas_call(functools.partial(hartree_kernel, group, unroll), out_shap...  46.7 us
    ppermute x6, waiting for transfers between devices, gather_xor(): lax.ppermute(out, axis, [(i, i ^ bit) for i in range(count)])  15.8 us
    ppermute x1, starting transfers between devices, body(): lax.ppermute(own, 'space', [(i + 1, i) for i in range(ends)])  4.54 us
    ppermute x2, starting transfers between devices, sum_xor(): lax.ppermute(value, axis, [(i, i ^ bit) for i in range(count)])  4.3 us
  transfers between devices with their start and end apart: 10, of which 7 were waited for; matrix products, arithmetic and copies ran while one was open for 1% of the time, Pallas kernels for 0%

profile of v1, /device:TPU:4, one launch (start us, length us, event | category | flops | bytes accessed | tf_op | source)
XLA Modules:
  0.0 188.8 jit_solution(13193017179909801191)
XLA Ops:
  0.6 0.0 copy-start.3
  0.6 0.9 multiply_reduce_fusion
  1.6 0.0 copy-start.8
  1.6 1.6 collective-permute-start.2
  3.2 0.0 copy-done.8
  3.2 0.0 copy-start.6
  3.2 0.0 copy-start.7
  3.2 0.0 copy-done.3
  3.2 0.0 copy-start.5
  3.3 0.7 copy-done.6
  4.0 0.0 copy-start.4
  4.0 0.0 copy-done.7
  4.0 0.1 concatenate.28.own
  4.1 1.9 %collective-permute-start = (f32[16,16,128]{2,1,0:T(8,128)S(1)}, f32[16,16,128]{2,1,0:T(8,128)S(1)}, u32[]{:S(2)}, u32[]{:S(2)}) collective-permute-start(f32[16,16,128]{2,1,0:T(8,128)S(1)} %concatenate.28.own), channel_id=1, source_target_pairs={{0,1},{1,2},{2,3},{3,4},{4,5},{5,6},{6,7},{8,9},{9,10},{10,11},{11... | collective-permute-start | bytes 393224 | tf_op jit(solution)/shard_map/ppermute | solution.py:324
  6.0 4.5 %collective-permute-start.1 = (f32[16,16,128]{2,1,0:T(8,128)S(1)}, f32[16,16,128]{2,1,0:T(8,128)S(1)}, u32[]{:S(2)}, u32[]{:S(2)}) collective-permute-start(f32[16,16,128]{2,1,0:T(8,128)S(1)} %concatenate.28.own), channel_id=1, source_target_pairs={{1,0},{2,1},{3,2},{4,3},{5,4},{6,5},{7,6},{9,8},{10,9},{11,10},{12... | collective-permute-start | bytes 393224 | tf_op jit(solution)/shard_map/ppermute | solution.py:326
  10.5 0.0 collective-permute-done.2
  10.6 2.7 %collective-permute-start.3 = (f32[16,128]{1,0:T(8,128)S(1)}, f32[16,128]{1,0:T(8,128)S(1)}, u32[]{:S(2)}, u32[]{:S(2)}) collective-permute-start(f32[16,128]{1,0:T(8,128)S(1)} %fusion), channel_id=1, source_target_pairs={{0,16},{8,24},{16,0},{24,8},{1,17},{9,25},{17,1},{25,9},{2,18},{10... | collective-permute-start | bytes 24584 | tf_op jit(solution)/shard_map/ppermute | solution.py:277
  13.2 0.0 copy-done.5
  13.2 0.0 copy-done.4
  13.2 0.0 copy-start
  13.3 1.9 %collective-permute-done.3 = f32[16,128]{1,0:T(8,128)S(1)} collective-permute-done((f32[16,128]{1,0:T(8,128)S(1)}, f32[16,128]{1,0:T(8,128)S(1)}, u32[]{:S(2)}, u32[]{:S(2)}) %collective-permute-start.3) | collective-permute-done | bytes 8224 | tf_op jit(solution)/shard_map/ppermute | solution.py:277
  15.2 0.0 copy-done
  15.2 0.0 copy-start.2
  15.2 0.4 charge.1
  15.7 0.0 collective-permute-start.4
  15.7 0.2 copy-done.2
  15.9 0.1 convert_reduce_fusion.1
  16.0 0.0 copy-start.1
  16.0 0.8 collective-permute-done.4
  16.9 0.6 collective-permute-start.5
  17.5 0.0 copy-done.1
  17.5 0.1 convert_reduce_fusion
  17.6 3.1 %collective-permute-done.5 = f32[2,24,128]{2,1,0:T(8,128)S(1)} collective-permute-done((f32[2,24,128]{2,1,0:T(8,128)S(1)}, f32[2,24,128]{2,1,0:T(8,128)S(1)}, u32[]{:S(2)}, u32[]{:S(2)}) %collective-permute-start.5) | collective-permute-done | bytes 24608 | tf_op jit(solution)/shard_map/ppermute | solution.py:268
  20.7 0.0 collective-permute-start.6
  20.7 0.1 copy.24.counts
  20.8 4.0 %collective-permute-done.6 = f32[4,24,128]{2,1,0:T(8,128)S(1)} collective-permute-done((f32[4,24,128]{2,1,0:T(8,128)S(1)}, f32[4,24,128]{2,1,0:T(8,128)S(1)}, u32[]{:S(2)}, u32[]{:S(2)}) %collective-permute-start.6) | collective-permute-done | bytes 49184 | tf_op jit(solution)/shard_map/ppermute | solution.py:268
  24.8 0.0 collective-permute-done
  24.8 0.0 collective-permute-done.1
  24.9 46.7 %hartree.1 = f32[24,128]{1,0:T(8,128)S(1)} custom-call(s32[1]{0:T(128)} %bitcast.meta, s32[16,2]{1,0:T(8,128)S(1)} %copy.24.counts, s32[16,27]{1,0:T(8,128)S(1)} %copy-done.2, s32[16,42]{1,0:T(8,128)S(1)} %copy-done.1, f32[12,8,128]{2,1,0:T(8,128)S(1)} %copy-done, f32[56,8,128]{2,1,0:T(8,128)S(1)} %multiply_add_fusion.table, ...), custom_call_target="tpu_custom_call" | custom-call | tf_op jit(solution)/shard_map/hartree/pallas_call | solution.py:353
  71.5 0.0 copy-start.9
  71.5 0.0 copy-start.10
  71.5 0.1 collective-permute-start.7
  71.6 1.2 collective-permute-done.7
  72.8 0.4 collective-permute-start.8
  73.2 0.0 copy-done.9
  73.2 0.0 copy-done.10
  73.2 0.2 select_reduce_fusion
  73.4 3.2 %collective-permute-done.8 = f32[2,24,128]{2,1,0:T(8,128)S(1)} collective-permute-done((f32[2,24,128]{2,1,0:T(8,128)S(1)}, f32[2,24,128]{2,1,0:T(8,128)S(1)}, u32[]{:S(2)}, u32[]{:S(2)}) %collective-permute-start.8) | collective-permute-done | bytes 24608 | tf_op jit(solution)/shard_map/ppermute | solution.py:268
  76.6 0.0 collective-permute-start.9
  76.7 0.6 slice.4
  77.3 3.5 %collective-permute-done.9 = f32[4,24,128]{2,1,0:T(8,128)S(1)} collective-permute-done((f32[4,24,128]{2,1,0:T(8,128)S(1)}, f32[4,24,128]{2,1,0:T(8,128)S(1)}, u32[]{:S(2)}, u32[]{:S(2)}) %collective-permute-start.9) | collective-permute-done | bytes 49184 | tf_op jit(solution)/shard_map/ppermute | solution.py:268
  80.7 108.1 %orbitals.1 = f32[8,16,128]{2,1,0:T(8,128)} custom-call(s32[1]{0:T(128)} %bitcast.meta, s32[16,2]{1,0:T(8,128)S(1)} %copy.24.counts, s32[16,27]{1,0:T(8,128)S(1)} %copy-done.2, s32[16,42]{1,0:T(8,128)S(1)} %copy-done.1, f32[8]{0:T(128)S(1)} %broadcast_multiply_fusion.2.rate, f32[12,8,128]{2,1,0:T(8,128)S(1)} %copy-done, ...), custom_call_target="tpu_custom_call" | custom-call | tf_op jit(solution)/shard_map/orbitals/pallas_call | solution.py:365
  (17 shorter events, 0.2 us)
Async XLA Ops:
  0.6 2.6 %copy-start.3 = (f32[8,16,128]{2,1,0:T(8,128)S(1)}, f32[8,16,128]{2,1,0:T(8,128)}, u32[]{:S(2)}) copy-start(f32[8,16,128]{2,1,0:T(8,128)} %param.11) | copy-start | bytes 196612
  1.6 1.7 copy-start.8
  1.6 9.0 %collective-permute-start.2 = (f32[16,128]{1,0:T(8,128)S(1)}, f32[16,128]{1,0:T(8,128)S(1)}, u32[]{:S(2)}, u32[]{:S(2)}) collective-permute-start(f32[16,128]{1,0:T(8,128)S(1)} %broadcast_multiply_fusion), channel_id=1, source_target_pairs={{0,8},{8,0},{16,24},{24,16},{1,9},{9,1},{17,25},{25,17},{2,10},{10... | collective-permute-start | bytes 24584 | tf_op jit(solution)/shard_map/ppermute | solution.py:277
  3.2 0.7 copy-start.6
  3.2 0.8 copy-start.7
  3.2 10.0 %copy-start.5 = (f32[56,8,128]{2,1,0:T(8,128)S(1)}, f32[56,8,128]{2,1,0:T(8,128)}, u32[]{:S(2)}) copy-start(f32[56,8,128]{2,1,0:T(8,128)} %constant.9.clone) | copy-start | bytes 688132
  4.0 9.3 %copy-start.4 = (f32[56,8,128]{2,1,0:T(8,128)S(1)}, f32[56,8,128]{2,1,0:T(8,128)}, u32[]{:S(2)}) copy-start(f32[56,8,128]{2,1,0:T(8,128)} %constant.28.clone) | copy-start | bytes 688132
  4.1 20.7 %collective-permute-start = (f32[16,16,128]{2,1,0:T(8,128)S(1)}, f32[16,16,128]{2,1,0:T(8,128)S(1)}, u32[]{:S(2)}, u32[]{:S(2)}) collective-permute-start(f32[16,16,128]{2,1,0:T(8,128)S(1)} %concatenate.28.own), channel_id=1, source_target_pairs={{0,1},{1,2},{2,3},{3,4},{4,5},{5,6},{6,7},{8,9},{9,10},{10,11},{11... | collective-permute-start | bytes 393224 | tf_op jit(solution)/shard_map/ppermute | solution.py:324
  6.0 18.8 %collective-permute-start.1 = (f32[16,16,128]{2,1,0:T(8,128)S(1)}, f32[16,16,128]{2,1,0:T(8,128)S(1)}, u32[]{:S(2)}, u32[]{:S(2)}) collective-permute-start(f32[16,16,128]{2,1,0:T(8,128)S(1)} %concatenate.28.own), channel_id=1, source_target_pairs={{1,0},{2,1},{3,2},{4,3},{5,4},{6,5},{7,6},{9,8},{10,9},{11,10},{12... | collective-permute-start | bytes 393224 | tf_op jit(solution)/shard_map/ppermute | solution.py:326
  10.6 4.6 %collective-permute-start.3 = (f32[16,128]{1,0:T(8,128)S(1)}, f32[16,128]{1,0:T(8,128)S(1)}, u32[]{:S(2)}, u32[]{:S(2)}) collective-permute-start(f32[16,128]{1,0:T(8,128)S(1)} %fusion), channel_id=1, source_target_pairs={{0,16},{8,24},{16,0},{24,8},{1,17},{9,25},{17,1},{25,9},{2,18},{10... | collective-permute-start | bytes 24584 | tf_op jit(solution)/shard_map/ppermute | solution.py:277
  13.2 2.0 %copy-start = (f32[12,8,128]{2,1,0:T(8,128)S(1)}, f32[12,8,128]{2,1,0:T(8,128)}, u32[]{:S(2)}) copy-start(f32[12,8,128]{2,1,0:T(8,128)} %constant.8.clone.cst) | copy-start | bytes 147460
  15.2 0.7 copy-start.2
  15.7 1.2 collective-permute-start.4
  16.0 1.4 copy-start.1
  16.9 3.8 %collective-permute-start.5 = (f32[2,24,128]{2,1,0:T(8,128)S(1)}, f32[2,24,128]{2,1,0:T(8,128)S(1)}, u32[]{:S(2)}, u32[]{:S(2)}) collective-permute-start(f32[2,24,128]{2,1,0:T(8,128)S(1)} %pad_maximum_fusion.5), channel_id=1, source_target_pairs={{0,2},{1,3},{2,0},{3,1},{4,6},{5,7},{6,4},{7,5},{8,10},{9,11},{10,... | collective-permute-start | bytes 73736 | tf_op jit(solution)/shard_map/ppermute | solution.py:268
  20.7 4.1 %collective-permute-start.6 = (f32[4,24,128]{2,1,0:T(8,128)S(1)}, f32[4,24,128]{2,1,0:T(8,128)S(1)}, u32[]{:S(2)}, u32[]{:S(2)}) collective-permute-start(f32[4,24,128]{2,1,0:T(8,128)S(1)} %pad_maximum_fusion.3), channel_id=1, source_target_pairs={{0,4},{1,5},{2,6},{3,7},{4,0},{5,1},{6,2},{7,3},{8,12},{9,13},{10,... | collective-permute-start | bytes 147464 | tf_op jit(solution)/shard_map/ppermute | solution.py:268
  71.5 1.7 copy-start.9
  71.5 1.7 copy-start.10
  71.5 1.3 collective-permute-start.7
  72.8 3.8 %collective-permute-start.8 = (f32[2,24,128]{2,1,0:T(8,128)S(1)}, f32[2,24,128]{2,1,0:T(8,128)S(1)}, u32[]{:S(2)}, u32[]{:S(2)}) collective-permute-start(f32[2,24,128]{2,1,0:T(8,128)S(1)} %pad_maximum_fusion.6), channel_id=1, source_target_pairs={{0,2},{1,3},{2,0},{3,1},{4,6},{5,7},{6,4},{7,5},{8,10},{9,11},{10,... | collective-permute-start | bytes 73736 | tf_op jit(solution)/shard_map/ppermute | solution.py:268
  76.6 4.1 %collective-permute-start.9 = (f32[4,24,128]{2,1,0:T(8,128)S(1)}, f32[4,24,128]{2,1,0:T(8,128)S(1)}, u32[]{:S(2)}, u32[]{:S(2)}) collective-permute-start(f32[4,24,128]{2,1,0:T(8,128)S(1)} %pad_maximum_fusion.4), channel_id=1, source_target_pairs={{0,4},{1,5},{2,6},{3,7},{4,0},{5,1},{6,2},{7,3},{8,12},{9,13},{10,... | collective-permute-start | bytes 147464 | tf_op jit(solution)/shard_map/ppermute | solution.py:268

commit v2 on v1

v2 whole, which is shorter than its diff:
```python
import functools
import math

import jax
import jax.numpy as jnp
import numpy as np
from jax import lax
from jax.experimental import pallas as pl
from jax.experimental.pallas import tpu as pltpu
from jax.sharding import PartitionSpec as P

NODES = 4
LANES = 128
PLANE = 16
ROWS = 8
HALF = NODES**3

cell_side = 0.25
soften = 6.25e-06
green_scale = -0.5 / math.pi
log2e = math.log2(math.e)
highest = lax.Precision.HIGHEST

node_set = np.cos((2.0 * np.arange(NODES) + 1.0) * (math.pi / (2.0 * NODES)))
roots = [[node_set[m] for m in range(NODES) if m != a] for a in range(NODES)]
scales = [1.0 / np.prod([node_set[a] - r for r in roots[a]]) for a in range(NODES)]


def basis_rows():
    row = np.arange(ROWS)
    out = []
    for pick in (row // 4, 2 + row // 4, row % 4):
        for k in range(NODES - 1):
            out.append([roots[a][k] for a in pick])
        out.append([scales[a] for a in pick])
    return np.broadcast_to(np.array(out, np.float32)[:, :, None], (12, ROWS, LANES)).copy()


def proxy_table(planes, window):
    offset = 0.5 * (node_set + 1.0)
    p = np.arange(LANES) % HALF
    offs = np.stack([offset[p // 16], offset[p // 4 % 4], offset[p % 4]])
    cells = np.arange(window)
    lows = np.stack([cells % 4, cells // 4 % 4, cells // 16]) * cell_side
    near = lows[:, :, None] + offs[:, None, :] * cell_side
    levels = np.arange(planes)
    lows = np.stack([0 * levels, 0 * levels, levels]) * cell_side
    far = lows[:, :, None] + offs[:, None, :] * np.array([1.0, 1.0, cell_side])[:, None, None]
    table = np.zeros((window + planes, ROWS, LANES), np.float32)
    table[:, :3] = np.moveaxis(np.concatenate([near, far], 1), 0, 1)
    return table


def poly(u, r0, r1, r2, scale):
    return ((u - r0) * (u - r1)) * ((u - r2) * scale)


def weights(cst, x, y, z, lows, sides):
    ux, uy, uz = (
        jnp.broadcast_to(2.0 * (c - lo) / e - 1.0, (ROWS, LANES)) for c, lo, e in zip((x, y, z), lows, sides)
    )
    pz = poly(uz, cst[8], cst[9], cst[10], cst[11])
    pyz = [poly(uy, cst[4 * k], cst[4 * k + 1], cst[4 * k + 2], cst[4 * k + 3]) * pz for k in range(2)]
    parts = []
    for a in range(NODES):
        px = poly(ux, *(float(r) for r in roots[a]), float(scales[a]))
        parts += [px * pyz[0], px * pyz[1]]
    return jnp.concatenate(parts + parts, axis=0)


def cell_low(cell):
    return [(cell % 4).astype(jnp.float32) * cell_side, (cell // 4 % 4).astype(jnp.float32) * cell_side]


def dot_nt(a, b):
    return lax.dot_general(a, b, (((1,), (1,)), ((), ())), precision=highest, preferred_element_type=jnp.float32)


def gather_xor(block, axis, pairs):
    count = lax.axis_size(axis)
    out = block[None]
    while out.shape[0] < count:
        have = out.shape[0]
        steps = range(1, 4 if (have > 1 or pairs) and have * 4 <= count else 2)
        parts = [lax.ppermute(out, axis, [(i, i ^ (have * j)) for i in range(count)]) for j in steps]
        out = jnp.concatenate([out] + parts, axis=0)
    return out


def target_cell(me, t, groups):
    return t * groups + lax.bitwise_xor(jnp.int32(t) if isinstance(t, int) else t, me)


def strided(phi, c, kinds):
    return phi[pl.ds(c, kinds, stride=PLANE), :]


def split(v):
    high = v.astype(jnp.bfloat16)
    return high, (v - high.astype(jnp.float32)).astype(jnp.bfloat16)


def dot_bf16(a, b):
    return lax.dot_general(a, b, (((1,), (1,)), ((), ())), preferred_element_type=jnp.float32)


def dot_split(v, w):
    vh, vl = split(v)
    wh, wl = split(w)
    rows = v.shape[0]
    both = dot_bf16(jnp.concatenate([vh, vl], axis=0), wh)
    return both[:rows] + both[rows:] + dot_bf16(vh, wl)


def charge_kernel(meta, cst, own, phi, out):
    z_low = meta[0].astype(jnp.float32) * cell_side
    groups = phi.shape[0]
    kinds = (phi.shape[1] - ROWS) // PLANE
    density = jnp.zeros((PLANE, LANES), jnp.float32)
    for g in range(groups):
        for j in range(kinds):
            v = phi[g, j * PLANE : (j + 1) * PLANE, :]
            density = density + v * v
    out[:PLANE, :] = density
    acc = jnp.zeros((LANES, LANES), jnp.float32)
    ones = jnp.ones((ROWS, LANES), jnp.float32)
    for c in range(PLANE):
        charge = own[c, 4:5, :] * (2.0 * out[c : c + 1, :])
        out[c : c + 1, :] = charge
        x, y, z = own[c, 0:1, :], own[c, 1:2, :], own[c, 2:3, :]
        low = (cell_side * (c % 4), cell_side * (c // 4), z_low)
        acc = acc + weights(cst, x, y, z, (0.0, 0.0, z_low), (1.0, 1.0, cell_side)) * charge
        moments = dot_nt(ones, weights(cst, x, y, z, low, (cell_side,) * 3) * charge)
        out[PLANE + c : PLANE + c + 1, :] = moments[0:1, :]
    out[2 * PLANE :, :] = dot_nt(ones, acc)


def live_planes(me, planes):
    below = jnp.maximum(me - 1, 0)
    return below, below + jnp.maximum(planes - 2 - me, 0)


def list_sources(me, cell, counts, near, far, planes, table, pts, src, put_near, put_far, put_none, multiple):
    window = 3 * PLANE
    base = (me - 1) * PLANE
    below, n_planes = live_planes(me, planes)
    low_half = lax.broadcasted_iota(jnp.int32, (1, LANES), 1) < HALF
    n_near, n_far = counts[cell, 0], counts[cell, 1]
    n_items = n_far + n_planes
    n_pairs = (n_items + 1) // 2

    def near_step(j, c):
        slot = near[cell, j] - base
        src[j] = pts[slot]
        put_near(j, slot)
        return c

    lax.fori_loop(0, n_near, near_step, 0)

    def item(j):
        j = jnp.minimum(j, n_items - 1)
        p = j - n_far
        level = jnp.where(p < below, p, p + (me + 2 - below))
        slot = far[cell, jnp.minimum(j, far.shape[1] - 1)] - base
        return jnp.where(j < n_far, slot, window + level)

    def far_step(j, c):
        first, second = item(2 * j), item(2 * j + 1)
        src[n_near + j] = jnp.where(low_half, table[first], table[second])
        put_far(n_near + j, first, second, 2 * j + 1 < n_items, low_half)
        return c

    lax.fori_loop(0, n_pairs, far_step, 0)
    n_blocks = n_near + n_pairs
    for u in range(multiple - 1):
        src[n_blocks + u] = jnp.zeros(src.shape[1:], jnp.float32)
        put_none(n_blocks + u)
    return n_blocks


def put_targets(pts, cell, tgt):
    for d in range(3):
        tgt[d] = jnp.broadcast_to(pts[PLANE + cell, d : d + 1, :], (LANES, LANES)).T


def square(tgt, src, slot, rows):
    dx = tgt[0, rows, :] - src[slot, 0:1, :]
    dy = tgt[1, rows, :] - src[slot, 1:2, :]
    dz = tgt[2, rows, :] - src[slot, 2:3, :]
    return (dx * dx + dy * dy) + (dz * dz + soften)


def hartree_kernel(unroll, meta, counts, near, far, cst, table, pts, phi, gathered, out, val, mom, tgt, src, srcv):
    planes = gathered.shape[0]
    groups = phi.shape[0]
    kinds = (phi.shape[1] - ROWS) // PLANE
    cells = PLANE // groups
    me, group = meta[0], meta[1]
    for k in range(3):
        there = lax.bitwise_xor(me, jnp.clip(me - 1 + k, 0, planes - 1))
        val[k * PLANE : (k + 1) * PLANE, 0, :] = gathered[there, :PLANE, :]
        mom[k * PLANE : (k + 1) * PLANE, 0, :] = gathered[there, PLANE : 2 * PLANE, :]

    def put_plane(g, c):
        mom[3 * PLANE + g] = gathered[lax.bitwise_xor(me, g), 2 * PLANE : 2 * PLANE + 1, :]
        return c

    lax.fori_loop(0, planes, put_plane, 0)

    def put_near(j, slot):
        srcv[j] = val[slot]

    def put_far(j, first, second, live, low_half):
        srcv[j] = jnp.where(low_half, mom[first], mom[second] * live.astype(jnp.float32))

    def put_none(j):
        srcv[j] = jnp.zeros((1, LANES), jnp.float32)

    z_low = me.astype(jnp.float32) * cell_side
    total = jnp.zeros((groups * kinds, LANES), jnp.float32)
    out[0] = jnp.zeros((ROWS, LANES), jnp.float32)
    for t in range(cells):
        cell = target_cell(group, t, groups)
        n_blocks = list_sources(
            me, cell, counts, near, far, planes, table, pts, src, put_near, put_far, put_none, unroll
        )
        put_targets(pts, cell, tgt)

        def step(k, acc):
            for u in range(unroll):
                slot = k * unroll + u
                acc = acc + lax.rsqrt(square(tgt, src, slot, slice(None))) * srcv[slot]
            return acc

        acc = lax.fori_loop(0, (n_blocks + unroll - 1) // unroll, step, jnp.zeros((LANES, LANES), jnp.float32))
        row = dot_nt(jnp.ones((ROWS, LANES), jnp.float32), acc)[0:1, :]
        out[0, t : t + 1, :] = row
        there = PLANE + cell
        scaled = pts[there, 4:5, :] * (pts[there, 3:4, :] + row)
        v = jnp.concatenate([strided(phi.at[k], cell, kinds) for k in range(groups)], axis=0) * scaled
        w = weights(
            cst, pts[there, 0:1, :], pts[there, 1:2, :], pts[there, 2:3, :], (0.0, 0.0, z_low), (1.0, 1.0, cell_side)
        )
        total = total + dot_split(v, w)
    for k in range(groups):
        out[1 + lax.bitwise_xor(group, k), :kinds, :] = total[k * kinds : (k + 1) * kinds, :]


def orbital_kernel(
    batch, meta, counts, near, far, levels, screening, cst, table, pts, phi, before, after, gathered,
    out, hartree, rate, slot_of, val, mom, tgt, src, srcv, dist, inv, even, odd, acc, total,
):
    planes = gathered.shape[0]
    groups, cells, kinds, _ = out.shape
    orbs = groups * kinds
    me, group = meta[0], meta[1]

    def clear(i, c):
        slot_of[i] = -1
        rate[i] = 0.0
        return c

    lax.fori_loop(0, screening.shape[0], clear, 0)
    for q in range(2 * batch):
        rate[screening.shape[0] + q] = 0.0
    lane = lax.broadcasted_iota(jnp.int32, (1, LANES), 1) % orbs

    def rank(i, carry):
        found, lane_slot = carry
        level = levels[i]
        known = slot_of[level]
        slot = jnp.where(known < 0, found, known)
        slot_of[level] = slot
        rate[slot] = screening[level] * (-log2e)
        return found + (known < 0).astype(jnp.int32), jnp.where(lane == i, slot, lane_slot)

    n_levels, lane_slot = lax.fori_loop(0, orbs, rank, (jnp.int32(0), jnp.zeros((1, LANES), jnp.int32)))
    n_batches = (n_levels + batch - 1) // batch

    for k in range(3):
        there = lax.bitwise_xor(me, jnp.clip(me - 1 + k, 0, planes - 1))
        field = (before, phi, after)[k]

        def prepare(c, carry):
            at = k * PLANE + c
            share = lax.rem(c, groups)
            owner = lax.bitwise_xor(lax.bitwise_xor(share, c // groups), group)
            potential = pts[at, 3:4, :] + gathered[there, owner, 0, pl.ds(c // groups, 1), :]
            scaled = pts[at, 4:5, :] * potential
            v = jnp.concatenate([strided(field.at[g], c, kinds) for g in range(groups)], axis=0) * scaled
            vh, vl = split(v)
            both = jnp.concatenate([vh, vl], axis=0)
            val[at] = both
            z_low = (me - 1 + k).astype(jnp.float32) * cell_side
            low = (*cell_low(c), z_low)
            wh, wl = split(weights(cst, pts[at, 0:1, :], pts[at, 1:2, :], pts[at, 2:3, :], low, (cell_side,) * 3))
            first = dot_bf16(both, wh)
            mh, ml = split(first[:orbs] + first[orbs:] + dot_bf16(vh, wl))
            mom[at] = jnp.concatenate([mh, ml], axis=0)
            return carry

        lax.fori_loop(0, PLANE, prepare, 0, unroll=4)

    def put_plane(g, c):
        there = lax.bitwise_xor(me, g)
        parts = []
        for k in range(groups):
            source = 1 + lax.bitwise_xor(group, k)
            parts.append(sum(gathered[there, z, source, :kinds, :] for z in range(groups)))
        mh, ml = split(jnp.concatenate(parts, axis=0))
        mom[3 * PLANE + g] = jnp.concatenate([mh, ml], axis=0)
        return c

    lax.fori_loop(0, planes, put_plane, 0)

    def put_near(j, slot):
        srcv[j] = val[slot]

    def put_far(j, first, second, live, low_half):
        srcv[j] = jnp.where(low_half, mom[first], jnp.where(live, mom[second], jnp.zeros_like(mom[second])))

    def put_none(j):
        srcv[j] = jnp.zeros(srcv.shape[1:], srcv.dtype)

    def make(ref, b, unit):
        rates = [rate[b * batch + q] for q in range(batch)]
        for half in range(2):
            for r in range(LANES // 16):
                rows = slice(16 * r, 16 * r + 16)
                d = dist[2 * unit + half, rows, :]
                i = inv[2 * unit + half, rows, :]
                for q in range(batch):
                    ref[q * LANES + 16 * r : q * LANES + 16 * r + 16, half * LANES : (half + 1) * LANES] = (
                        jnp.exp2(d * rates[q]) * i
                    ).astype(jnp.bfloat16)

    def consume(ref, unit):
        v = jnp.concatenate([srcv[2 * unit], srcv[2 * unit + 1]], axis=1)
        acc[...] = acc[...] + dot_bf16(ref[...], v)

    def per_cell(t, carry):
        cell = target_cell(group, t, groups)
        n_blocks = list_sources(me, cell, counts, near, far, planes, table, pts, src, put_near, put_far, put_none, 4)
        n_loops = (n_blocks + 3) // 4
        put_targets(pts, cell, tgt)

        def measure(c, x):
            sq = square(tgt, src, c, slice(None))
            i = lax.rsqrt(sq)
            inv[c] = i
            dist[c] = sq * i
            return x

        lax.fori_loop(0, 4 * n_loops, measure, 0)
        total[...] = jnp.zeros(total.shape, jnp.float32)
        make(even, 0, 0)

        def per_batch(b, x):
            acc[...] = jnp.zeros(acc.shape, jnp.float32)

            def step(i, y):
                make(odd, b, 2 * i + 1)
                consume(even, 2 * i)
                last = i + 1 == n_loops
                make(even, jnp.where(last, b + 1, b), jnp.where(last, 0, 2 * i + 2))
                consume(odd, 2 * i + 1)
                return y

            lax.fori_loop(0, n_loops, step, 0)
            add = total[...]
            for q in range(batch):
                mine = lane_slot[:, : 2 * orbs] == b * batch + q
                add = add + jnp.where(mine, acc[q * LANES : (q + 1) * LANES, :], 0.0)
            total[...] = add
            return x

        lax.fori_loop(0, n_batches, per_batch, 0)
        flipped = jnp.concatenate([total[...], jnp.zeros((LANES, LANES - 2 * orbs), jnp.float32)], axis=1).T
        rows = (flipped[:orbs] + flipped[orbs : 2 * orbs]) * green_scale
        for k in range(groups):
            out[k, t] = rows[k * kinds : (k + 1) * kinds]
        return carry

    lax.fori_loop(0, cells, per_cell, 0)
    for k in range(groups):
        for t in range(cells):
            cell = target_cell(lax.bitwise_xor(group, k), t, groups)
            hartree[pl.ds(cell, 1), :] = gathered[0, k, 0, t : t + 1, :]


def place_kernel(meta, *refs):
    parts, out, ordered = refs[:-2], refs[-2], refs[-1]
    for k, part in enumerate(parts):
        for t in range(part.shape[0]):
            ordered[target_cell(lax.bitwise_xor(meta[1], k), t, len(parts))] = part[t]
    for c in range(PLANE):
        out[:, c, :] = ordered[c]


def smem():
    return pl.BlockSpec(memory_space=pltpu.SMEM)


def vmem():
    return pl.BlockSpec(memory_space=pltpu.VMEM)


def call(kernel, name, out_shape, smems, args, scratch=()):
    return pl.pallas_call(
        kernel,
        out_shape=out_shape,
        in_specs=[smem()] * smems + [vmem()] * (len(args) - smems),
        out_specs=jax.tree.map(lambda _: vmem(), out_shape),
        scratch_shapes=scratch,
        compiler_params=pltpu.CompilerParams(vmem_limit_bytes=52 * 1024 * 1024),
        name=name,
    )(*args)


def body(orbitals, points, quad_weight, external, screening, level_index, near_cells, far_cells):
    kinds, cells, point_count = orbitals.shape
    planes, groups = lax.axis_size("space"), lax.axis_size("orb")
    orbs = kinds * groups
    window = 3 * PLANE
    share = cells // groups
    me, group = lax.axis_index("space"), lax.axis_index("orb")
    meta = jnp.stack([me, group]).astype(jnp.int32)
    f32, bf16 = jnp.float32, jnp.bfloat16

    marks = jnp.broadcast_to(level_index.astype(f32)[:, None], (kinds, LANES))
    phi = jnp.concatenate(
        [orbitals.reshape(kinds * cells, LANES), marks, jnp.zeros((ROWS - kinds, LANES), f32)], axis=0
    )
    phi = gather_xor(phi, "orb", True)
    weight = quad_weight * (cell_side**3 / point_count)
    own = jnp.concatenate(
        [jnp.transpose(points, (1, 0, 2)), external[:, None], weight[:, None], jnp.zeros((cells, 3, LANES), f32)], axis=1
    )
    ends = planes - 1
    up = [(i, i + 1) for i in range(ends)]
    down = [(i + 1, i) for i in range(ends)]
    pts = jnp.concatenate([lax.ppermute(own, "space", up), own, lax.ppermute(own, "space", down)], axis=0)
    cst = jnp.asarray(basis_rows())
    base_table = proxy_table(planes, window)
    shift = np.zeros(base_table.shape, np.float32)
    shift[:window, 2] = cell_side
    table = jnp.asarray(base_table) + jnp.asarray(shift) * (me - 1).astype(f32)
    counts = jnp.stack(
        [jnp.sum((near_cells >= 0).astype(jnp.int32), 1), jnp.sum((far_cells >= 0).astype(jnp.int32), 1)], axis=1
    )
    levels = phi[:, kinds * cells : kinds * cells + kinds, 0].reshape(orbs).astype(jnp.int32)

    charges = call(
        charge_kernel, "charge", jax.ShapeDtypeStruct((2 * cells + ROWS, LANES), f32), 1, (meta, cst, own, phi)
    )
    charges = gather_xor(charges, "space", False)
    before, after = lax.ppermute(phi, "space", up), lax.ppermute(phi, "space", down)

    unroll = 2
    blocks = near_cells.shape[1] + (far_cells.shape[1] + planes + 1) // 2 + 6
    shares = call(
        functools.partial(hartree_kernel, unroll),
        "hartree",
        jax.ShapeDtypeStruct((1 + groups, ROWS, LANES), f32),
        4,
        (meta, counts, near_cells, far_cells, cst, table, pts, phi, charges),
        [
            pltpu.VMEM((window, 1, LANES), f32),
            pltpu.VMEM((window + planes, 1, LANES), f32),
            pltpu.VMEM((3, LANES, LANES), f32),
            pltpu.VMEM((blocks, ROWS, LANES), f32),
            pltpu.VMEM((blocks, 1, LANES), f32),
        ],
    )
    gathered = gather_xor(gather_xor(shares, "orb", True), "space", False)

    batch = 4
    sent, hartree = call(
        functools.partial(orbital_kernel, batch),
        "orbitals",
        (jax.ShapeDtypeStruct((groups, share, kinds, LANES), f32), jax.ShapeDtypeStruct((cells, LANES), f32)),
        6,
        (meta, counts, near_cells, far_cells, levels, screening, cst, table, pts, phi, before, after, gathered),
        [
            pltpu.SMEM((screening.shape[0] + 2 * batch,), f32),
            pltpu.SMEM((screening.shape[0],), jnp.int32),
            pltpu.VMEM((window, 2 * orbs, LANES), bf16),
            pltpu.VMEM((window + planes, 2 * orbs, LANES), bf16),
            pltpu.VMEM((3, LANES, LANES), f32),
            pltpu.VMEM((blocks, ROWS, LANES), f32),
            pltpu.VMEM((blocks, 2 * orbs, LANES), bf16),
            pltpu.VMEM((blocks, LANES, LANES), f32),
            pltpu.VMEM((blocks, LANES, LANES), f32),
            pltpu.VMEM((batch * LANES, 2 * LANES), bf16),
            pltpu.VMEM((batch * LANES, 2 * LANES), bf16),
            pltpu.VMEM((batch * LANES, 2 * orbs), f32),
            pltpu.VMEM((LANES, 2 * orbs), f32),
        ],
    )
    parts = [sent[0]]
    for k in range(1, groups):
        parts.append(lax.ppermute(sent[k], "orb", [(i, i ^ k) for i in range(groups)]))
    updated = call(
        place_kernel,
        "place",
        jax.ShapeDtypeStruct((kinds, cells, LANES), f32),
        1,
        (meta, *parts),
        [pltpu.VMEM((cells, kinds, LANES), f32)],
    )
    return updated, hartree


def solution(mesh):
    in_specs = (
        P("orb", "space", None),
        P(None, "space", None),
        P("space", None),
        P("space", None),
        P(),
        P("orb"),
        P("space", None),
        P("space", None),
    )
    out_specs = (P("orb", "space", None), P("space", None))
    return jax.shard_map(body, mesh=mesh, in_specs=in_specs, out_specs=out_specs, check_vma=False)
```

time: 189 us -> 179 us (0.947); the launches traced: 189 us -> 177 us
  Pallas kernels: 155 us -> 110 us
  starting transfers between devices: 11.9 us -> 39 us
  other arithmetic: 1.43 us -> 3.89 us
  local copies, waits for them, and re-layouts: 1.75 us -> 3.84 us
    pallas_call x3 -> x4, Pallas kernels: 155 us -> 110 us  [call(): pl.pallas_call(kernel, out_shape=out_shape, in_specs=[smem()] * smems + [...]
    ppermute x10 -> x21, starting transfers between devices: 11.9 us -> 39 us  [the longest x14 16.6 us: gather_xor(): lax.ppermute(out, axis, [(i, i ^ have * j) for i in range(count)])]
    unnamed x24 -> x22, local copies, waits for them, and re-layouts: 1 us -> 3.63 us
    ppermute x10 -> x21, waiting for transfers between devices: 17.7 us -> 19 us  [the longest x14 13.4 us: gather_xor(): lax.ppermute(out, axis, [(i, i ^ have * j) for i in range(count)])]
  transfers between devices with their start and end apart: 10 -> 21, of which waited for: 7 -> 9; matrix products, arithmetic and copies ran while one was open for 1% -> 2% of each run, Pallas kernels for 0% -> 0%
where the time goes in v2:
time: 179 us; the launch traced here: 177 us
  Pallas kernels  110 us (61%)
  starting transfers between devices  39 us (22%)
  waiting for transfers between devices  19 us (11%)
  other arithmetic  3.89 us (2%)
  local copies, waits for them, and re-layouts  3.84 us (2%)
    pallas_call x4, Pallas kernels, call(): pl.pallas_call(kernel, out_shape=out_shape, in_specs=[smem()] * smems + [...  110 us
    ppermute x14, starting transfers between devices, gather_xor(): lax.ppermute(out, axis, [(i, i ^ have * j) for i in range(count)])  16.6 us
    ppermute x14, waiting for transfers between devices, gather_xor(): lax.ppermute(out, axis, [(i, i ^ have * j) for i in range(count)])  13.4 us
    ppermute x3, starting transfers between devices, body(): lax.ppermute(sent[k], 'orb', [(i, i ^ k) for i in range(groups)])  9.45 us
    ppermute x3, waiting for transfers between devices, body(): lax.ppermute(sent[k], 'orb', [(i, i ^ k) for i in range(groups)])  5.53 us
    ppermute x1, starting transfers between devices, body(): lax.ppermute(own, 'space', down)  4.54 us
    ppermute x1, starting transfers between devices, body(): lax.ppermute(phi, 'space', down)  4.54 us
    unnamed x22, local copies, waits for them, and re-layouts  3.63 us
  transfers between devices with their start and end apart: 21, of which 9 were waited for; matrix products, arithmetic and copies ran while one was open for 2% of the time, Pallas kernels for 0%

profile of v2, /device:TPU:4, one launch (start us, length us, event | category | flops | bytes accessed | tf_op | source)
XLA Modules:
  0.0 176.7 jit_solution(1213420934713790405)
XLA Ops:
  0.6 0.0 copy-start.5
  0.6 0.7 convert_element_type.19
  1.4 0.9 maximum_bitcast_fusion.1
  2.3 1.6 collective-permute-start
  3.9 2.6 %collective-permute-start.1 = (f32[1,136,128]{2,1,0:T(8,128)S(1)}, f32[1,136,128]{2,1,0:T(8,128)S(1)}, u32[]{:S(2)}, u32[]{:S(2)}) collective-permute-start(f32[1,136,128]{2,1,0:T(8,128)S(1)} %maximum_bitcast_fusion.1), channel_id=1, source_target_pairs={{0,16},{8,24},{16,0},{24,8},{1,17},{9,25},{17,1},{25,9},{2,18},{10... | collective-permute-start | bytes 208904 | tf_op jit(solution)/shard_map/ppermute | solution.py:85
  6.5 0.2 collective-permute-start.2
  6.7 0.8 copy.23
  7.5 0.7 broadcast_multiply_fusion
  8.2 0.7 copy-done.6
  8.9 0.0 copy-start.2
  8.9 1.9 %collective-permute-start.3 = (f32[16,8,128]{2,1,0:T(8,128)S(1)}, f32[16,8,128]{2,1,0:T(8,128)S(1)}, u32[]{:S(2)}, u32[]{:S(2)}) collective-permute-start(f32[16,8,128]{2,1,0:T(8,128)S(1)} %pad_maximum_fusion.3.own), channel_id=1, source_target_pairs={{0,1},{1,2},{2,3},{3,4},{4,5},{5,6},{6,7},{8,9},{9,10},{10,11},{11... | collective-permute-start | bytes 196616 | tf_op jit(solution)/shard_map/ppermute | solution.py:442
  10.9 4.5 %collective-permute-start.4 = (f32[16,8,128]{2,1,0:T(8,128)S(1)}, f32[16,8,128]{2,1,0:T(8,128)S(1)}, u32[]{:S(2)}, u32[]{:S(2)}) collective-permute-start(f32[16,8,128]{2,1,0:T(8,128)S(1)} %pad_maximum_fusion.3.own), channel_id=1, source_target_pairs={{1,0},{2,1},{3,2},{4,3},{5,4},{6,5},{7,6},{9,8},{10,9},{11,10},{12... | collective-permute-start | bytes 196616 | tf_op jit(solution)/shard_map/ppermute | solution.py:442
  15.4 0.0 copy-start.1
  15.4 0.1 convert_reduce_fusion.1
  15.6 0.6 copy-done.1
  16.1 0.1 convert_reduce_fusion
  16.2 0.1 copy.21.counts
  16.3 1.0 multiply_add_fusion.table
  17.3 0.1 pad_add_fusion.1.meta
  17.4 0.0 collective-permute-done.3
  17.4 0.0 collective-permute-done.4
  17.4 0.0 copy-start
  17.4 0.0 collective-permute-done
  17.5 0.0 collective-permute-done.2
  17.5 0.7 copy-done
  18.2 2.4 %charge.1 = f32[40,128]{1,0:T(8,128)S(1)} custom-call(s32[2]{0:T(128)S(1)} %pad_add_fusion.1.meta, f32[12,8,128]{2,1,0:T(8,128)S(1)} %copy-done, f32[16,8,128]{2,1,0:T(8,128)S(1)} %pad_maximum_fusion.3.own, f32[4,136,128]{2,1,0:T(8,128)S(1)} %pad_maximum_fusion.phi), custom_call_target="tpu_custom_call" | custom-call | tf_op jit(solution)/shard_map/charge/pallas_call | solution.py:409
  20.6 0.7 collective-permute-start.7
  21.3 0.8 collective-permute-done.7
  22.2 0.3 collective-permute-start.8
  22.5 2.6 %collective-permute-start.9 = (f32[2,40,128]{2,1,0:T(8,128)S(1)}, f32[2,40,128]{2,1,0:T(8,128)S(1)}, u32[]{:S(2)}, u32[]{:S(2)}) collective-permute-start(f32[2,40,128]{2,1,0:T(8,128)S(1)} %pad_maximum_fusion.4), channel_id=1, source_target_pairs={{0,4},{1,5},{2,6},{3,7},{4,0},{5,1},{6,2},{7,3},{8,12},{9,13},{10,... | collective-permute-start | bytes 122888 | tf_op jit(solution)/shard_map/ppermute | solution.py:85
  25.1 0.6 collective-permute-start.10
  25.7 0.5 collective-permute-done.8
  26.2 0.9 collective-permute-done.9
  27.1 2.9 %collective-permute-done.10 = f32[2,40,128]{2,1,0:T(8,128)S(1)} collective-permute-done((f32[2,40,128]{2,1,0:T(8,128)S(1)}, f32[2,40,128]{2,1,0:T(8,128)S(1)}, u32[]{:S(2)}, u32[]{:S(2)}) %collective-permute-start.10) | collective-permute-done | bytes 40992 | tf_op jit(solution)/shard_map/ppermute | solution.py:85
  30.0 9.3 %hartree.1 = f32[5,8,128]{2,1,0:T(8,128)S(1)} custom-call(s32[2]{0:T(128)S(1)} %pad_add_fusion.1.meta, s32[16,2]{1,0:T(8,128)S(1)} %copy.21.counts, s32[16,27]{1,0:T(8,128)S(1)} %copy-done.2, s32[16,42]{1,0:T(8,128)S(1)} %copy-done.1, f32[12,8,128]{2,1,0:T(8,128)S(1)} %copy-done, f32[56,8,128]{2,1,0:T(8,128)S(1)} %multiply_add_fusion.table, ...), custom_call_target="tpu_custom_call" | custom-call | tf_op jit(solution)/shard_map/hartree/pallas_call | solution.py:409
  39.2 0.7 collective-permute-start.11
  39.9 3.7 %collective-permute-start.12 = (f32[1,5,8,128]{3,2,1,0:T(8,128)S(1)}, f32[1,5,8,128]{3,2,1,0:T(8,128)S(1)}, u32[]{:S(2)}, u32[]{:S(2)}) collective-permute-start(f32[1,5,8,128]{3,2,1,0:T(8,128)S(1)} %bitcast.30), channel_id=1, source_target_pairs={{0,16},{8,24},{16,0},{24,8},{1,17},{9,25},{17,1},{25,9},{2,18},{10... | collective-permute-start | bytes 61448 | tf_op jit(solution)/shard_map/ppermute | solution.py:85
  43.6 0.1 collective-permute-start.13
  43.7 1.9 %collective-permute-start.5 = (f32[4,136,128]{2,1,0:T(8,128)S(1)}, f32[4,136,128]{2,1,0:T(8,128)S(1)}, u32[]{:S(2)}, u32[]{:S(2)}) collective-permute-start(f32[4,136,128]{2,1,0:T(8,128)S(1)} %pad_maximum_fusion.phi), channel_id=1, source_target_pairs={{0,1},{1,2},{2,3},{3,4},{4,5},{5,6},{6,7},{8,9},{9,10},{10,11},{11... | collective-permute-start | bytes 835592 | tf_op jit(solution)/shard_map/ppermute | solution.py:457
  45.6 4.5 %collective-permute-start.6 = (f32[4,136,128]{2,1,0:T(8,128)S(1)}, f32[4,136,128]{2,1,0:T(8,128)S(1)}, u32[]{:S(2)}, u32[]{:S(2)}) collective-permute-start(f32[4,136,128]{2,1,0:T(8,128)S(1)} %pad_maximum_fusion.phi), channel_id=1, source_target_pairs={{1,0},{2,1},{3,2},{4,3},{5,4},{6,5},{7,6},{9,8},{10,9},{11,10},{12... | collective-permute-start | bytes 835592 | tf_op jit(solution)/shard_map/ppermute | solution.py:457
  50.1 0.0 collective-permute-done.11
  50.1 0.0 collective-permute-done.13
  50.2 0.1 collective-permute-start.14
  50.2 0.1 fusion
  50.4 0.1 convert_element_type.21.levels
  50.5 1.0 collective-permute-done.14
  51.5 0.1 collective-permute-start.15
  51.6 0.7 collective-permute-start.16
  52.3 2.8 %collective-permute-start.17 = (f32[2,4,5,8,128]{4,3,2,1,0:T(8,128)S(1)}, f32[2,4,5,8,128]{4,3,2,1,0:T(8,128)S(1)}, u32[]{:S(2)}, u32[]{:S(2)}) collective-permute-start(f32[2,4,5,8,128]{4,3,2,1,0:T(8,128)S(1)} %pad_maximum_fusion.2), channel_id=1, source_target_pairs={{0,6},{1,7},{2,4},{3,5},{4,2},{5,3},{6,0},{7,1},{8,14},{9,15},{10,... | collective-permute-start | bytes 491528 | tf_op jit(solution)/shard_map/ppermute | solution.py:85
  55.1 4.3 %collective-permute-done.15 = f32[2,4,5,8,128]{4,3,2,1,0:T(8,128)S(1)} collective-permute-done((f32[2,4,5,8,128]{4,3,2,1,0:T(8,128)S(1)}, f32[2,4,5,8,128]{4,3,2,1,0:T(8,128)S(1)}, u32[]{:S(2)}, u32[]{:S(2)}) %collective-permute-start.15) | collective-permute-done | bytes 163872 | tf_op jit(solution)/shard_map/ppermute | solution.py:85
  59.4 0.0 collective-permute-done.16
  59.5 0.0 copy-start.3
  59.5 2.9 %collective-permute-done.17 = f32[2,4,5,8,128]{4,3,2,1,0:T(8,128)S(1)} collective-permute-done((f32[2,4,5,8,128]{4,3,2,1,0:T(8,128)S(1)}, f32[2,4,5,8,128]{4,3,2,1,0:T(8,128)S(1)}, u32[]{:S(2)}, u32[]{:S(2)}) %collective-permute-start.17) | collective-permute-done | bytes 163872 | tf_op jit(solution)/shard_map/ppermute | solution.py:85
  62.4 0.0 collective-permute-done.5.before
  62.5 0.0 collective-permute-done.6.after
  62.5 0.8 copy-done.4
  63.3 97.1 %orbitals.1 = (f32[4,4,8,128]{3,2,1,0:T(8,128)S(1)}, f32[16,128]{1,0:T(8,128)}) custom-call(s32[2]{0:T(128)S(1)} %pad_add_fusion.1.meta, s32[16,2]{1,0:T(8,128)S(1)} %copy.21.counts, s32[16,27]{1,0:T(8,128)S(1)} %copy-done.2, s32[16,42]{1,0:T(8,128)S(1)} %copy-done.1, s32[32]{0:T(128)S(1)} %convert_element_type.21.levels, f32[32]{0:T(128)S(1)} %copy-done.3, ...), custom_call_target="tpu_custom_call" | custom-call | tf_op jit(solution)/shard_map/orbitals/pallas_call | solution.py:409
  160.4 3.1 %collective-permute-start.18 = (f32[4,8,128]{2,1,0:T(8,128)S(1)}, f32[4,8,128]{2,1,0:T(8,128)S(1)}, u32[]{:S(2)}, u32[]{:S(2)}) collective-permute-start(f32[4,8,128]{2,1,0:T(8,128)S(1)} %get-tuple-element.8), channel_id=1, source_target_pairs={{0,8},{8,0},{16,24},{24,16},{1,9},{9,1},{17,25},{25,17},{2,10},{10... | collective-permute-start | bytes 49160 | tf_op jit(solution)/shard_map/ppermute | solution.py:502
  163.6 6.3 %collective-permute-start.19 = (f32[4,8,128]{2,1,0:T(8,128)S(1)}, f32[4,8,128]{2,1,0:T(8,128)S(1)}, u32[]{:S(2)}, u32[]{:S(2)}) collective-permute-start(f32[4,8,128]{2,1,0:T(8,128)S(1)} %get-tuple-element.7), channel_id=1, source_target_pairs={{0,16},{8,24},{16,0},{24,8},{1,17},{9,25},{17,1},{25,9},{2,18},{10... | collective-permute-start | bytes 49160 | tf_op jit(solution)/shard_map/ppermute | solution.py:502
  169.9 0.0 collective-permute-start.20
  169.9 0.0 collective-permute-done.18.refs_1_
  169.9 1.7 collective-permute-done.19.refs_2_
  171.6 3.8 %collective-permute-done.20.refs_3_ = f32[4,8,128]{2,1,0:T(8,128)S(1)} collective-permute-done((f32[4,8,128]{2,1,0:T(8,128)S(1)}, f32[4,8,128]{2,1,0:T(8,128)S(1)}, u32[]{:S(2)}, u32[]{:S(2)}) %collective-permute-start.20) | collective-permute-done | bytes 16416 | tf_op jit(solution)/shard_map/ppermute | solution.py:502
  175.4 1.2 place.1
  (27 shorter events, 0.3 us)
Async XLA Ops:
  0.6 15.7 %copy-start.5 = (f32[56,8,128]{2,1,0:T(8,128)S(1)}, f32[56,8,128]{2,1,0:T(8,128)}, u32[]{:S(2)}) copy-start(f32[56,8,128]{2,1,0:T(8,128)} %constant.26.clone) | copy-start | bytes 688132
  2.3 15.2 %collective-permute-start = (f32[1,136,128]{2,1,0:T(8,128)S(1)}, f32[1,136,128]{2,1,0:T(8,128)S(1)}, u32[]{:S(2)}, u32[]{:S(2)}) collective-permute-start(f32[1,136,128]{2,1,0:T(8,128)S(1)} %maximum_bitcast_fusion.1), channel_id=1, source_target_pairs={{0,8},{8,0},{16,24},{24,16},{1,9},{9,1},{17,25},{25,17},{2,10},{10... | collective-permute-start | bytes 208904 | tf_op jit(solution)/shard_map/ppermute | solution.py:85
  3.9 13.5 %collective-permute-start.1 = (f32[1,136,128]{2,1,0:T(8,128)S(1)}, f32[1,136,128]{2,1,0:T(8,128)S(1)}, u32[]{:S(2)}, u32[]{:S(2)}) collective-permute-start(f32[1,136,128]{2,1,0:T(8,128)S(1)} %maximum_bitcast_fusion.1), channel_id=1, source_target_pairs={{0,16},{8,24},{16,0},{24,8},{1,17},{9,25},{17,1},{25,9},{2,18},{10... | collective-permute-start | bytes 208904 | tf_op jit(solution)/shard_map/ppermute | solution.py:85
  6.5 11.0 %collective-permute-start.2 = (f32[1,136,128]{2,1,0:T(8,128)S(1)}, f32[1,136,128]{2,1,0:T(8,128)S(1)}, u32[]{:S(2)}, u32[]{:S(2)}) collective-permute-start(f32[1,136,128]{2,1,0:T(8,128)S(1)} %maximum_bitcast_fusion.1), channel_id=1, source_target_pairs={{0,24},{8,16},{16,8},{24,0},{1,25},{9,17},{17,9},{25,1},{2,26},{10... | collective-permute-start | bytes 208904 | tf_op jit(solution)/shard_map/ppermute | solution.py:85
  8.2 0.7 copy-start.6
  8.9 6.5 %copy-start.2 = (s32[16,27]{1,0:T(8,128)S(1)}, s32[16,27]{1,0:T(8,128)}, u32[]{:S(2)}) copy-start(s32[16,27]{1,0:T(8,128)} %near.3) | copy-start | bytes 5188
  8.9 8.4 %collective-permute-start.3 = (f32[16,8,128]{2,1,0:T(8,128)S(1)}, f32[16,8,128]{2,1,0:T(8,128)S(1)}, u32[]{:S(2)}, u32[]{:S(2)}) collective-permute-start(f32[16,8,128]{2,1,0:T(8,128)S(1)} %pad_maximum_fusion.3.own), channel_id=1, source_target_pairs={{0,1},{1,2},{2,3},{3,4},{4,5},{5,6},{6,7},{8,9},{9,10},{10,11},{11... | collective-permute-start | bytes 196616 | tf_op jit(solution)/shard_map/ppermute | solution.py:442
  10.9 6.5 %collective-permute-start.4 = (f32[16,8,128]{2,1,0:T(8,128)S(1)}, f32[16,8,128]{2,1,0:T(8,128)S(1)}, u32[]{:S(2)}, u32[]{:S(2)}) collective-permute-start(f32[16,8,128]{2,1,0:T(8,128)S(1)} %pad_maximum_fusion.3.own), channel_id=1, source_target_pairs={{1,0},{2,1},{3,2},{4,3},{5,4},{6,5},{7,6},{9,8},{10,9},{11,10},{12... | collective-permute-start | bytes 196616 | tf_op jit(solution)/shard_map/ppermute | solution.py:442
  15.4 0.7 copy-start.1
  17.4 0.8 copy-start
  20.6 1.5 collective-permute-start.7
  22.2 4.0 %collective-permute-start.8 = (f32[2,40,128]{2,1,0:T(8,128)S(1)}, f32[2,40,128]{2,1,0:T(8,128)S(1)}, u32[]{:S(2)}, u32[]{:S(2)}) collective-permute-start(f32[2,40,128]{2,1,0:T(8,128)S(1)} %pad_maximum_fusion.4), channel_id=1, source_target_pairs={{0,2},{1,3},{2,0},{3,1},{4,6},{5,7},{6,4},{7,5},{8,10},{9,11},{10,... | collective-permute-start | bytes 122888 | tf_op jit(solution)/shard_map/ppermute | solution.py:85
  22.5 4.6 %collective-permute-start.9 = (f32[2,40,128]{2,1,0:T(8,128)S(1)}, f32[2,40,128]{2,1,0:T(8,128)S(1)}, u32[]{:S(2)}, u32[]{:S(2)}) collective-permute-start(f32[2,40,128]{2,1,0:T(8,128)S(1)} %pad_maximum_fusion.4), channel_id=1, source_target_pairs={{0,4},{1,5},{2,6},{3,7},{4,0},{5,1},{6,2},{7,3},{8,12},{9,13},{10,... | collective-permute-start | bytes 122888 | tf_op jit(solution)/shard_map/ppermute | solution.py:85
  25.1 4.9 %collective-permute-start.10 = (f32[2,40,128]{2,1,0:T(8,128)S(1)}, f32[2,40,128]{2,1,0:T(8,128)S(1)}, u32[]{:S(2)}, u32[]{:S(2)}) collective-permute-start(f32[2,40,128]{2,1,0:T(8,128)S(1)} %pad_maximum_fusion.4), channel_id=1, source_target_pairs={{0,6},{1,7},{2,4},{3,5},{4,2},{5,3},{6,0},{7,1},{8,14},{9,15},{10,... | collective-permute-start | bytes 122888 | tf_op jit(solution)/shard_map/ppermute | solution.py:85
  39.2 10.9 %collective-permute-start.11 = (f32[1,5,8,128]{3,2,1,0:T(8,128)S(1)}, f32[1,5,8,128]{3,2,1,0:T(8,128)S(1)}, u32[]{:S(2)}, u32[]{:S(2)}) collective-permute-start(f32[1,5,8,128]{3,2,1,0:T(8,128)S(1)} %bitcast.29), channel_id=1, source_target_pairs={{0,8},{8,0},{16,24},{24,16},{1,9},{9,1},{17,25},{25,17},{2,10},{10... | collective-permute-start | bytes 61448 | tf_op jit(solution)/shard_map/ppermute | solution.py:85
  39.9 10.2 %collective-permute-start.12 = (f32[1,5,8,128]{3,2,1,0:T(8,128)S(1)}, f32[1,5,8,128]{3,2,1,0:T(8,128)S(1)}, u32[]{:S(2)}, u32[]{:S(2)}) collective-permute-start(f32[1,5,8,128]{3,2,1,0:T(8,128)S(1)} %bitcast.30), channel_id=1, source_target_pairs={{0,16},{8,24},{16,0},{24,8},{1,17},{9,25},{17,1},{25,9},{2,18},{10... | collective-permute-start | bytes 61448 | tf_op jit(solution)/shard_map/ppermute | solution.py:85
  43.6 6.6 %collective-permute-start.13 = (f32[1,5,8,128]{3,2,1,0:T(8,128)S(1)}, f32[1,5,8,128]{3,2,1,0:T(8,128)S(1)}, u32[]{:S(2)}, u32[]{:S(2)}) collective-permute-start(f32[1,5,8,128]{3,2,1,0:T(8,128)S(1)} %bitcast.31), channel_id=1, source_target_pairs={{0,24},{8,16},{16,8},{24,0},{1,25},{9,17},{17,9},{25,1},{2,26},{10... | collective-permute-start | bytes 61448 | tf_op jit(solution)/shard_map/ppermute | solution.py:85
  43.7 18.8 %collective-permute-start.5 = (f32[4,136,128]{2,1,0:T(8,128)S(1)}, f32[4,136,128]{2,1,0:T(8,128)S(1)}, u32[]{:S(2)}, u32[]{:S(2)}) collective-permute-start(f32[4,136,128]{2,1,0:T(8,128)S(1)} %pad_maximum_fusion.phi), channel_id=1, source_target_pairs={{0,1},{1,2},{2,3},{3,4},{4,5},{5,6},{6,7},{8,9},{9,10},{10,11},{11... | collective-permute-start | bytes 835592 | tf_op jit(solution)/shard_map/ppermute | solution.py:457
  45.6 16.9 %collective-permute-start.6 = (f32[4,136,128]{2,1,0:T(8,128)S(1)}, f32[4,136,128]{2,1,0:T(8,128)S(1)}, u32[]{:S(2)}, u32[]{:S(2)}) collective-permute-start(f32[4,136,128]{2,1,0:T(8,128)S(1)} %pad_maximum_fusion.phi), channel_id=1, source_target_pairs={{1,0},{2,1},{3,2},{4,3},{5,4},{6,5},{7,6},{9,8},{10,9},{11,10},{12... | collective-permute-start | bytes 835592 | tf_op jit(solution)/shard_map/ppermute | solution.py:457
  50.2 1.3 collective-permute-start.14
  51.5 7.9 %collective-permute-start.15 = (f32[2,4,5,8,128]{4,3,2,1,0:T(8,128)S(1)}, f32[2,4,5,8,128]{4,3,2,1,0:T(8,128)S(1)}, u32[]{:S(2)}, u32[]{:S(2)}) collective-permute-start(f32[2,4,5,8,128]{4,3,2,1,0:T(8,128)S(1)} %pad_maximum_fusion.2), channel_id=1, source_target_pairs={{0,2},{1,3},{2,0},{3,1},{4,6},{5,7},{6,4},{7,5},{8,10},{9,11},{10,... | collective-permute-start | bytes 491528 | tf_op jit(solution)/shard_map/ppermute | solution.py:85
  51.6 7.8 %collective-permute-start.16 = (f32[2,4,5,8,128]{4,3,2,1,0:T(8,128)S(1)}, f32[2,4,5,8,128]{4,3,2,1,0:T(8,128)S(1)}, u32[]{:S(2)}, u32[]{:S(2)}) collective-permute-start(f32[2,4,5,8,128]{4,3,2,1,0:T(8,128)S(1)} %pad_maximum_fusion.2), channel_id=1, source_target_pairs={{0,4},{1,5},{2,6},{3,7},{4,0},{5,1},{6,2},{7,3},{8,12},{9,13},{10,... | collective-permute-start | bytes 491528 | tf_op jit(solution)/shard_map/ppermute | solution.py:85
  52.3 10.1 %collective-permute-start.17 = (f32[2,4,5,8,128]{4,3,2,1,0:T(8,128)S(1)}, f32[2,4,5,8,128]{4,3,2,1,0:T(8,128)S(1)}, u32[]{:S(2)}, u32[]{:S(2)}) collective-permute-start(f32[2,4,5,8,128]{4,3,2,1,0:T(8,128)S(1)} %pad_maximum_fusion.2), channel_id=1, source_target_pairs={{0,6},{1,7},{2,4},{3,5},{4,2},{5,3},{6,0},{7,1},{8,14},{9,15},{10,... | collective-permute-start | bytes 491528 | tf_op jit(solution)/shard_map/ppermute | solution.py:85
  59.5 3.8 %copy-start.3 = (f32[32]{0:T(128)S(1)}, f32[32]{0:T(128)}, u32[]{:S(2)}) copy-start(f32[32]{0:T(128)} %screening.1) | copy-start | bytes 388
  62.4 0.9 copy-start.4
  160.4 9.5 %collective-permute-start.18 = (f32[4,8,128]{2,1,0:T(8,128)S(1)}, f32[4,8,128]{2,1,0:T(8,128)S(1)}, u32[]{:S(2)}, u32[]{:S(2)}) collective-permute-start(f32[4,8,128]{2,1,0:T(8,128)S(1)} %get-tuple-element.8), channel_id=1, source_target_pairs={{0,8},{8,0},{16,24},{24,16},{1,9},{9,1},{17,25},{25,17},{2,10},{10... | collective-permute-start | bytes 49160 | tf_op jit(solution)/shard_map/ppermute | solution.py:502
  163.6 8.1 %collective-permute-start.19 = (f32[4,8,128]{2,1,0:T(8,128)S(1)}, f32[4,8,128]{2,1,0:T(8,128)S(1)}, u32[]{:S(2)}, u32[]{:S(2)}) collective-permute-start(f32[4,8,128]{2,1,0:T(8,128)S(1)} %get-tuple-element.7), channel_id=1, source_target_pairs={{0,16},{8,24},{16,0},{24,8},{1,17},{9,25},{17,1},{25,9},{2,18},{10... | collective-permute-start | bytes 49160 | tf_op jit(solution)/shard_map/ppermute | solution.py:502
  169.9 5.5 %collective-permute-start.20 = (f32[4,8,128]{2,1,0:T(8,128)S(1)}, f32[4,8,128]{2,1,0:T(8,128)S(1)}, u32[]{:S(2)}, u32[]{:S(2)}) collective-permute-start(f32[4,8,128]{2,1,0:T(8,128)S(1)} %get-tuple-element.6), channel_id=1, source_target_pairs={{0,24},{8,16},{16,8},{24,0},{1,25},{9,17},{17,9},{25,1},{2,26},{10... | collective-permute-start | bytes 49160 | tf_op jit(solution)/shard_map/ppermute | solution.py:502
